TPU v7x, 256 devices: a whole 4x4x8 slice. The times are simulated.
256 devices in a mesh: gx: 8 (over z), gy: 8 (over y, core), gz: 4 (over x).
Axes of the slice: x: 4, y: 4, z: 8, core: 2. Of those that a mesh axis runs over, the one named last changes fastest.
Arguments:
- source: float32 [32, 256, 1024], P('gz', 'gx', 'gy'), may hold values from -8 to 8
- permeability: float32 [32, 256, 1024], P('gz', 'gx', 'gy'), may hold values from 0.01 to 100
- storage: float32 [32, 256, 1024], P('gz', 'gx', 'gy'), may hold values from 0.01 to 0.2
- column_depth: int32 [256, 1024], P('gx', 'gy'), may hold values from 16 to 32
Outputs:
- pressure: float32 [32, 256, 1024], P('gz', 'gx', 'gy')
- history: float32 [3], replicated
Inputs may be any that keep to these rules, and one draw needn't show every extreme that they name: A cell (z, x, y) is active when z < column_depth[x, y].
All inputs are finite; a program needn't handle non-finite values.
Results may differ from a plain program's by a relative error of at most 0.0001.
Values sent between devices are 32-bit elements; how exact they have to be, the bound alone decides.
A program may use at most 64 MiB of HBM per device.

v0:
```python
import jax
import jax.numpy as jnp
from jax import lax
from jax.sharding import PartitionSpec as P

ITERS = 3
SWEEPS = 4


RELAXATION = 0.9
NEIGHBOURS = (
    (slice(0, -2), slice(1, -1), slice(1, -1)),
    (slice(2, None), slice(1, -1), slice(1, -1)),
    (slice(1, -1), slice(0, -2), slice(1, -1)),
    (slice(1, -1), slice(2, None), slice(1, -1)),
    (slice(1, -1), slice(1, -1), slice(0, -2)),
    (slice(1, -1), slice(1, -1), slice(2, None)),
)


def extended(x, sides, width):
    for axis, dim in sides:
        size, length = (lax.axis_size(axis), x.shape[dim])
        up = [(i, (i + 1) % size) for i in range(size - 1)]
        down = [(j, i) for i, j in up]
        last = lax.slice_in_dim(x, length - width, length, axis=dim)
        leading = lax.slice_in_dim(x, 0, width, axis=dim)
        before = lax.ppermute(last, axis, up)
        after = lax.ppermute(leading, axis, down)
        x = jnp.concatenate([before, x, after], axis=dim)
    return x


def prepare(widened):
    perm_all = widened[0]
    active_all = widened[1]
    centre_perm = perm_all[1:-1, 1:-1, 1:-1]
    centre_active = active_all[1:-1, 1:-1, 1:-1]
    couplings = []
    for neighbour in NEIGHBOURS:
        other_perm = perm_all[neighbour]
        other_active = active_all[neighbour]
        couplings.append(
            centre_active
            * other_active
            * 2.0
            * centre_perm
            * other_perm
            / (centre_perm + other_perm + (1.0 - centre_active) + (1.0 - other_active))
        )
    diagonal = widened[2][1:-1, 1:-1, 1:-1] + (1.0 - centre_active)
    for coupling in couplings:
        diagonal = diagonal + coupling
    return (couplings, diagonal)


def apply_operator(field_wide, couplings, diagonal):
    result = diagonal * field_wide[1:-1, 1:-1, 1:-1]
    for coupling, neighbour in zip(couplings, NEIGHBOURS):
        result = result - coupling * field_wide[neighbour]
    return result


def local_solve(couplings, diagonal, residual_block):
    correction = jnp.zeros_like(residual_block)
    for sweep_step in range(SWEEPS):
        widened = jnp.pad(correction, 1)
        correction = (
            correction
            + RELAXATION
            * (residual_block - apply_operator(widened, couplings, diagonal))
            / diagonal
        )
    return correction


def multiplicity(position, owner, owners, extent):
    lower_edge = jnp.logical_and(position < 2, owner > 0)
    upper_edge = jnp.logical_and(position >= extent - 2, owner < owners - 1)
    return 1.0 + lower_edge.astype(jnp.float32) + upper_edge.astype(jnp.float32)


def axis_count(extent, owner, owners):
    position = jnp.arange(extent, dtype=jnp.int32)
    return multiplicity(position, owner, owners, extent)


def edge_layers(field, axis_dim):
    extent = field.shape[axis_dim]
    return jnp.concatenate(
        [
            lax.slice_in_dim(field, 0, 2, axis=axis_dim),
            lax.slice_in_dim(field, extent - 2, extent, axis=axis_dim),
        ],
        axis_dim,
    )


def absorb(field, arrived, axis_dim):
    extent = field.shape[axis_dim]
    interior = lax.slice_in_dim(field, 2, extent - 2, axis=axis_dim)
    inner_extent = extent - 4
    lower_edge = lax.slice_in_dim(interior, 0, 2, axis=axis_dim) + lax.slice_in_dim(
        arrived, 0, 2, axis=axis_dim
    )
    middle = lax.slice_in_dim(interior, 2, inner_extent - 2, axis=axis_dim)
    upper_edge = lax.slice_in_dim(
        interior, inner_extent - 2, inner_extent, axis=axis_dim
    ) + lax.slice_in_dim(arrived, 6, 8, axis=axis_dim)
    return jnp.concatenate([lower_edge, middle, upper_edge], axis_dim)


def per_device(source, permeability, storage, column_depth):
    depth_cells, row_cells, column_cells = source.shape
    layers = lax.axis_index("gz") * depth_cells + jnp.arange(depth_cells, dtype=jnp.int32)
    active = (layers[:, None, None] < column_depth[None, :, :]).astype(jnp.float32)
    stacked = jnp.stack([permeability, active, storage, source])
    widened_stack = extended(stacked, (("gx", 2), ("gy", 3), ("gz", 1)), 3)
    inner_couplings, inner_diagonal = prepare(widened_stack[:, 2:-2, 2:-2, 2:-2])
    block_couplings, block_diagonal = prepare(widened_stack)
    covered = (
        axis_count(depth_cells, lax.axis_index("gz"), lax.axis_size("gz"))[:, None, None]
        * axis_count(row_cells, lax.axis_index("gx"), lax.axis_size("gx"))[None, :, None]
        * axis_count(column_cells, lax.axis_index("gy"), lax.axis_size("gy"))[None, None, :]
    )
    pressure = jnp.zeros_like(source)
    norm_terms = []
    for iteration in range(ITERS + 1):
        widened_pressure = extended(pressure, (("gx", 1), ("gy", 2), ("gz", 0)), 1)
        residual = active * (
            source - apply_operator(widened_pressure, inner_couplings, inner_diagonal)
        )
        local_square = jnp.sum(residual * residual)
        norm_terms.append(lax.psum(local_square, ("gx", "gy", "gz")))
        if iteration == ITERS:
            break
        residual_block = extended(residual, (("gx", 1), ("gy", 2), ("gz", 0)), 2)
        correction = local_solve(block_couplings, block_diagonal, residual_block)
        arrived = extended(edge_layers(correction, 0), (("gz", 0),), 2)
        correction = absorb(correction, arrived, 0)
        arrived = extended(edge_layers(correction, 1), (("gx", 1),), 2)
        correction = absorb(correction, arrived, 1)
        arrived = extended(edge_layers(correction, 2), (("gy", 2),), 2)
        correction = absorb(correction, arrived, 2)
        pressure = pressure + correction / covered
    squares = jnp.stack(norm_terms)
    history = jnp.sqrt(squares[1:] / squares[0])
    return (pressure, history)


def solution(mesh):
    placed = (P("gz", "gx", "gy"), P("gz", "gx", "gy"), P("gz", "gx", "gy"), P("gx", "gy"))
    return jax.shard_map(
        per_device,
        mesh=mesh,
        in_specs=placed,
        out_specs=(P("gz", "gx", "gy"), P()),
        check_vma=False,
    )
```

profile of v0, /device:TPU:1, one launch (start us, length us, event | category | flops | bytes accessed | tf_op | source)
XLA Modules:
  0.0 424.7 jit_solution(6766994950371884405)
XLA Ops:
  2.3 4.4 %collective-permute-start = (f32[4,8,3,128]{3,1,2,0:T(8,128)S(1)}, f32[4,8,3,128]{3,1,2,0:T(8,128)S(1)}, u32[]{:S(2)}, u32[]{:S(2)}) collective-permute-start(f32[4,8,3,128]{3,1,2,0:T(8,128)S(1)} %copy.313), channel_id=1, source_target_pairs={{0,32},{32,64},{64,96},{96,128},{128,160},{160,192},{192,224},{1,3... | collective-permute-start | bytes 147464 | tf_op jit(solution)/shard_map/ppermute | solution.py:28
  8.0 4.2 collective-permute-start.6
  15.3 4.4 %collective-permute-start.2 = (f32[4,8,38,3]{2,1,3,0:T(8,128)S(1)}, f32[4,8,38,3]{2,1,3,0:T(8,128)S(1)}, u32[]{:S(2)}, u32[]{:S(2)}) collective-permute-start(f32[4,8,38,3]{2,1,3,0:T(8,128)S(1)} %copy.293), channel_id=1, source_target_pairs={{0,4},{4,8},{8,12},{12,16},{16,20},{20,24},{24,28},{1,5},{5,9},{9,... | collective-permute-start | bytes 43784 | tf_op jit(solution)/shard_map/ppermute | solution.py:28
  36.0 4.7 %collective-permute-done.9 = f32[8,34,1]{2,1,0:T(8,128)S(1)} collective-permute-done((f32[8,34,1]{2,1,0:T(8,128)S(1)}, f32[8,34,1]{2,1,0:T(8,128)S(1)}, u32[]{:S(2)}, u32[]{:S(2)}) %collective-permute-start.9) | collective-permute-done | bytes 1120 | tf_op jit(solution)/shard_map/ppermute | solution.py:29
  40.8 4.0 collective-permute-start.10
  51.8 4.3 %collective-permute-start.12 = (f32[8,2,128]{2,1,0:T(2,128)S(1)}, f32[8,2,128]{2,1,0:T(2,128)S(1)}, u32[]{:S(2)}, u32[]{:S(2)}) collective-permute-start(f32[8,2,128]{2,1,0:T(2,128)S(1)} %get-tuple-element.101), channel_id=1, source_target_pairs={{0,32},{32,64},{64,96},{96,128},{128,160},{160,192},{192,224},{1,3... | collective-permute-start | bytes 24584 | tf_op jit(solution)/shard_map/ppermute | solution.py:28
  57.3 4.3 %collective-permute-done.13 = f32[8,2,128]{2,1,0:T(2,128)S(1)} collective-permute-done((f32[8,2,128]{2,1,0:T(2,128)S(1)}, f32[8,2,128]{2,1,0:T(2,128)S(1)}, u32[]{:S(2)}, u32[]{:S(2)}) %collective-permute-start.13) | collective-permute-done | bytes 8224 | tf_op jit(solution)/shard_map/ppermute | solution.py:29
  61.8 4.3 %collective-permute-start.14 = (f32[8,36,2]{2,1,0:T(8,128)S(1)}, f32[8,36,2]{2,1,0:T(8,128)S(1)}, u32[]{:S(2)}, u32[]{:S(2)}) collective-permute-start(f32[8,36,2]{2,1,0:T(8,128)S(1)} %get-tuple-element.87), channel_id=1, source_target_pairs={{0,4},{4,8},{8,12},{12,16},{16,20},{20,24},{24,28},{1,5},{5,9},{9,... | collective-permute-start | bytes 6920 | tf_op jit(solution)/shard_map/ppermute | solution.py:28
  68.3 4.4 %collective-permute-done.15 = f32[8,36,2]{2,1,0:T(8,128)S(1)} collective-permute-done((f32[8,36,2]{2,1,0:T(8,128)S(1)}, f32[8,36,2]{2,1,0:T(8,128)S(1)}, u32[]{:S(2)}, u32[]{:S(2)}) %collective-permute-start.15) | collective-permute-done | bytes 2336 | tf_op jit(solution)/shard_map/ppermute | solution.py:29
  77.4 3.7 collective-permute-done.17
  81.2 3.7 multiply_divide_fusion.2
  88.2 3.5 collective-permute-start.18
  96.4 4.0 collective-permute-done.19
  101.3 4.8 %collective-permute-start.20 = (f32[8,2,132]{2,0,1:T(8,128)S(1)}, f32[8,2,132]{2,0,1:T(8,128)S(1)}, u32[]{:S(2)}, u32[]{:S(2)}) collective-permute-start(f32[8,2,132]{2,0,1:T(8,128)S(1)} %copy.301), channel_id=1, source_target_pairs={{0,32},{32,64},{64,96},{96,128},{128,160},{160,192},{192,224},{1,3... | collective-permute-start | bytes 25352 | tf_op jit(solution)/shard_map/ppermute | solution.py:28
  108.5 4.6 %collective-permute-done.21 = f32[8,2,132]{2,0,1:T(8,128)S(1)} collective-permute-done((f32[8,2,132]{2,0,1:T(8,128)S(1)}, f32[8,2,132]{2,0,1:T(8,128)S(1)}, u32[]{:S(2)}, u32[]{:S(2)}) %collective-permute-start.21) | collective-permute-done | bytes 8480 | tf_op jit(solution)/shard_map/ppermute | solution.py:29
  115.5 7.2 %collective-permute-start.22 = (f32[8,32,2]{2,1,0:T(8,128)}, f32[8,32,2]{2,1,0:T(8,128)}, u32[]{:S(2)}, u32[]{:S(2)}) collective-permute-start(f32[8,32,2]{2,1,0:T(8,128)} %slice.988), channel_id=1, source_target_pairs={{0,4},{4,8},{8,12},{12,16},{16,20},{20,24},{24,28},{1,5},{5,9},{9,... | collective-permute-start | bytes 6152 | tf_op jit(solution)/shard_map/ppermute | solution.py:28
  129.0 4.1 collective-permute-done.23
  134.2 4.8 %collective-permute-start.24 = (f32[8,1,128]{2,1,0:T(1,128)S(1)}, f32[8,1,128]{2,1,0:T(1,128)S(1)}, u32[]{:S(2)}, u32[]{:S(2)}) collective-permute-start(f32[8,1,128]{2,1,0:T(1,128)S(1)} %get-tuple-element.99), channel_id=1, source_target_pairs={{0,32},{32,64},{64,96},{96,128},{128,160},{160,192},{192,224},{1,3... | collective-permute-start | bytes 12296 | tf_op jit(solution)/shard_map/ppermute | solution.py:28
  140.4 3.6 collective-permute-done.25
  149.4 4.4 %collective-permute-done.27 = f32[8,34,1]{2,1,0:T(8,128)S(1)} collective-permute-done((f32[8,34,1]{2,1,0:T(8,128)S(1)}, f32[8,34,1]{2,1,0:T(8,128)S(1)}, u32[]{:S(2)}, u32[]{:S(2)}) %collective-permute-start.27) | collective-permute-done | bytes 1120 | tf_op jit(solution)/shard_map/ppermute | solution.py:29
  153.9 3.6 collective-permute-start.28
  158.9 3.4 collective-permute-done.29
  163.5 4.8 %collective-permute-start.30 = (f32[8,2,128]{2,1,0:T(2,128)S(1)}, f32[8,2,128]{2,1,0:T(2,128)S(1)}, u32[]{:S(2)}, u32[]{:S(2)}) collective-permute-start(f32[8,2,128]{2,1,0:T(2,128)S(1)} %get-tuple-element.97), channel_id=1, source_target_pairs={{0,32},{32,64},{64,96},{96,128},{128,160},{160,192},{192,224},{1,3... | collective-permute-start | bytes 24584 | tf_op jit(solution)/shard_map/ppermute | solution.py:28
  173.1 4.3 %collective-permute-start.32 = (f32[8,36,2]{2,1,0:T(8,128)S(1)}, f32[8,36,2]{2,1,0:T(8,128)S(1)}, u32[]{:S(2)}, u32[]{:S(2)}) collective-permute-start(f32[8,36,2]{2,1,0:T(8,128)S(1)} %get-tuple-element.83), channel_id=1, source_target_pairs={{0,4},{4,8},{8,12},{12,16},{16,20},{20,24},{24,28},{1,5},{5,9},{9,... | collective-permute-start | bytes 6920 | tf_op jit(solution)/shard_map/ppermute | solution.py:28
  179.7 4.4 %collective-permute-done.33 = f32[8,36,2]{2,1,0:T(8,128)S(1)} collective-permute-done((f32[8,36,2]{2,1,0:T(8,128)S(1)}, f32[8,36,2]{2,1,0:T(8,128)S(1)}, u32[]{:S(2)}, u32[]{:S(2)}) %collective-permute-start.33) | collective-permute-done | bytes 2336 | tf_op jit(solution)/shard_map/ppermute | solution.py:29
  187.6 3.7 collective-permute-done.35
  198.2 4.3 %collective-permute-done.37 = f32[2,36,132]{2,1,0:T(8,128)S(1)} collective-permute-done((f32[2,36,132]{2,1,0:T(8,128)S(1)}, f32[2,36,132]{2,1,0:T(8,128)S(1)}, u32[]{:S(2)}, u32[]{:S(2)}) %collective-permute-start.37) | collective-permute-done | bytes 38048 | tf_op jit(solution)/shard_map/ppermute | solution.py:29
  202.5 3.6 collective-permute-start.38
  208.3 3.4 collective-permute-done.39
  211.9 8.0 %collective-permute-start.40 = (f32[8,32,2]{2,1,0:T(8,128)S(1)}, f32[8,32,2]{2,1,0:T(8,128)S(1)}, u32[]{:S(2)}, u32[]{:S(2)}) collective-permute-start(f32[8,32,2]{2,1,0:T(8,128)S(1)} %slice.1007), channel_id=1, source_target_pairs={{0,4},{4,8},{8,12},{12,16},{16,20},{20,24},{24,28},{1,5},{5,9},{9,... | collective-permute-start | bytes 6152 | tf_op jit(solution)/shard_map/ppermute | solution.py:28
  224.0 5.0 %collective-permute-done.41 = f32[8,32,2]{2,1,0:T(8,128)S(1)} collective-permute-done((f32[8,32,2]{2,1,0:T(8,128)S(1)}, f32[8,32,2]{2,1,0:T(8,128)S(1)}, u32[]{:S(2)}, u32[]{:S(2)}) %collective-permute-start.41) | collective-permute-done | bytes 2080 | tf_op jit(solution)/shard_map/ppermute | solution.py:29
  229.1 3.6 collective-permute-start.42
  242.7 4.4 %collective-permute-done.45 = f32[8,34,1]{2,1,0:T(8,128)S(1)} collective-permute-done((f32[8,34,1]{2,1,0:T(8,128)S(1)}, f32[8,34,1]{2,1,0:T(8,128)S(1)}, u32[]{:S(2)}, u32[]{:S(2)}) %collective-permute-start.45) | collective-permute-done | bytes 1120 | tf_op jit(solution)/shard_map/ppermute | solution.py:29
  247.2 3.4 collective-permute-start.46
  251.9 3.4 collective-permute-done.47
  264.5 4.4 %collective-permute-start.50 = (f32[8,36,2]{2,1,0:T(8,128)S(1)}, f32[8,36,2]{2,1,0:T(8,128)S(1)}, u32[]{:S(2)}, u32[]{:S(2)}) collective-permute-start(f32[8,36,2]{2,1,0:T(8,128)S(1)} %get-tuple-element.79), channel_id=1, source_target_pairs={{0,4},{4,8},{8,12},{12,16},{16,20},{20,24},{24,28},{1,5},{5,9},{9,... | collective-permute-start | bytes 6920 | tf_op jit(solution)/shard_map/ppermute | solution.py:28
  271.1 4.4 %collective-permute-done.51 = f32[8,36,2]{2,1,0:T(8,128)S(1)} collective-permute-done((f32[8,36,2]{2,1,0:T(8,128)S(1)}, f32[8,36,2]{2,1,0:T(8,128)S(1)}, u32[]{:S(2)}, u32[]{:S(2)}) %collective-permute-start.51) | collective-permute-done | bytes 2336 | tf_op jit(solution)/shard_map/ppermute | solution.py:29
  278.7 3.7 collective-permute-done.53
  289.2 4.2 collective-permute-done.55
  293.5 3.6 collective-permute-start.56
  299.4 3.4 collective-permute-done.57
  302.9 7.5 %collective-permute-start.58 = (f32[8,32,2]{2,1,0:T(8,128)S(1)}, f32[8,32,2]{2,1,0:T(8,128)S(1)}, u32[]{:S(2)}, u32[]{:S(2)}) collective-permute-start(f32[8,32,2]{2,1,0:T(8,128)S(1)} %slice.1026), channel_id=1, source_target_pairs={{0,4},{4,8},{8,12},{12,16},{16,20},{20,24},{24,28},{1,5},{5,9},{9,... | collective-permute-start | bytes 6152 | tf_op jit(solution)/shard_map/ppermute | solution.py:28
  314.5 5.0 %collective-permute-done.59 = f32[8,32,2]{2,1,0:T(8,128)S(1)} collective-permute-done((f32[8,32,2]{2,1,0:T(8,128)S(1)}, f32[8,32,2]{2,1,0:T(8,128)S(1)}, u32[]{:S(2)}, u32[]{:S(2)}) %collective-permute-start.59) | collective-permute-done | bytes 2080 | tf_op jit(solution)/shard_map/ppermute | solution.py:29
  319.7 3.6 collective-permute-start.60
  333.3 4.4 %collective-permute-done.63 = f32[8,34,1]{2,1,0:T(8,128)S(1)} collective-permute-done((f32[8,34,1]{2,1,0:T(8,128)S(1)}, f32[8,34,1]{2,1,0:T(8,128)S(1)}, u32[]{:S(2)}, u32[]{:S(2)}) %collective-permute-start.63) | collective-permute-done | bytes 1120 | tf_op jit(solution)/shard_map/ppermute | solution.py:29
  337.8 3.6 collective-permute-start.64
  342.8 3.4 collective-permute-done.65
  347.2 74.4 %all-reduce.12 = (f32[1]{0:T(128)}, f32[1]{0:T(128)}, f32[1]{0:T(128)}, f32[]{:T(128)}) all-reduce(f32[1]{0:T(128)} %bitcast.11, f32[1]{0:T(128)} %bitcast.10, f32[1]{0:T(128)} %bitcast.9, f32[]{:T(128)} %get-tuple-element.12), channel_id=1, replica_groups=mesh['gx'=8,'gy'=8,'gz'=4] {'gx','gy','gz'}, use_global_device_ids=true, to_apply=%region_5.6 | all-reduce | flops 4 | bytes 32 | tf_op jit(solution)/shard_map/psum | solution.py:134
  (243 shorter events, 146.0 us)
Async XLA Ops:
  2.3 11.2 %collective-permute-start = (f32[4,8,3,128]{3,1,2,0:T(8,128)S(1)}, f32[4,8,3,128]{3,1,2,0:T(8,128)S(1)}, u32[]{:S(2)}, u32[]{:S(2)}) collective-permute-start(f32[4,8,3,128]{3,1,2,0:T(8,128)S(1)} %copy.313), channel_id=1, source_target_pairs={{0,32},{32,64},{64,96},{96,128},{128,160},{160,192},{192,224},{1,3... | collective-permute-start | bytes 147464 | tf_op jit(solution)/shard_map/ppermute | solution.py:28
  6.7 6.8 %collective-permute-start.1 = (f32[4,8,3,128]{3,1,2,0:T(8,128)S(1)}, f32[4,8,3,128]{3,1,2,0:T(8,128)S(1)}, u32[]{:S(2)}, u32[]{:S(2)}) collective-permute-start(f32[4,8,3,128]{3,1,2,0:T(8,128)S(1)} %copy.314), channel_id=1, source_target_pairs={{32,0},{64,32},{96,64},{128,96},{160,128},{192,160},{224,192},{33,... | collective-permute-start | bytes 147464 | tf_op jit(solution)/shard_map/ppermute | solution.py:29
  8.0 13.9 %collective-permute-start.6 = (f32[8,1,128]{2,1,0:T(1,128)S(1)}, f32[8,1,128]{2,1,0:T(1,128)S(1)}, u32[]{:S(2)}, u32[]{:S(2)}) collective-permute-start(f32[8,1,128]{2,1,0:T(1,128)S(1)} %broadcast.159), channel_id=1, source_target_pairs={{0,32},{32,64},{64,96},{96,128},{128,160},{160,192},{192,224},{1,3... | collective-permute-start | bytes 12296 | tf_op jit(solution)/shard_map/ppermute | solution.py:28
  12.2 9.8 %collective-permute-start.7 = (f32[8,1,128]{2,1,0:T(1,128)S(1)}, f32[8,1,128]{2,1,0:T(1,128)S(1)}, u32[]{:S(2)}, u32[]{:S(2)}) collective-permute-start(f32[8,1,128]{2,1,0:T(1,128)S(1)} %broadcast.159), channel_id=1, source_target_pairs={{32,0},{64,32},{96,64},{128,96},{160,128},{192,160},{224,192},{33,... | collective-permute-start | bytes 12296 | tf_op jit(solution)/shard_map/ppermute | solution.py:29
  15.3 6.7 %collective-permute-start.2 = (f32[4,8,38,3]{2,1,3,0:T(8,128)S(1)}, f32[4,8,38,3]{2,1,3,0:T(8,128)S(1)}, u32[]{:S(2)}, u32[]{:S(2)}) collective-permute-start(f32[4,8,38,3]{2,1,3,0:T(8,128)S(1)} %copy.293), channel_id=1, source_target_pairs={{0,4},{4,8},{8,12},{12,16},{16,20},{20,24},{24,28},{1,5},{5,9},{9,... | collective-permute-start | bytes 43784 | tf_op jit(solution)/shard_map/ppermute | solution.py:28
  20.0 5.4 %collective-permute-start.3 = (f32[4,8,38,3]{2,1,3,0:T(8,128)S(1)}, f32[4,8,38,3]{2,1,3,0:T(8,128)S(1)}, u32[]{:S(2)}, u32[]{:S(2)}) collective-permute-start(f32[4,8,38,3]{2,1,3,0:T(8,128)S(1)} %copy.294), channel_id=1, source_target_pairs={{4,0},{8,4},{12,8},{16,12},{20,16},{24,20},{28,24},{5,1},{9,5},{13... | collective-permute-start | bytes 43784 | tf_op jit(solution)/shard_map/ppermute | solution.py:29
  26.8 19.3 %collective-permute-start.4 = (f32[4,3,38,134]{3,0,2,1:T(4,128)S(1)}, f32[4,3,38,134]{3,0,2,1:T(4,128)S(1)}, u32[]{:S(2)}, u32[]{:S(2)}) collective-permute-start(f32[4,3,38,134]{3,0,2,1:T(4,128)S(1)} %copy.297), channel_id=1, source_target_pairs={{0,1},{1,2},{2,3},{4,5},{5,6},{6,7},{8,9},{9,10},{10,11},{12,13},{... | collective-permute-start | bytes 733256 | tf_op jit(solution)/shard_map/ppermute | solution.py:28
  30.1 16.1 %collective-permute-start.5 = (f32[4,3,38,134]{3,0,2,1:T(4,128)S(1)}, f32[4,3,38,134]{3,0,2,1:T(4,128)S(1)}, u32[]{:S(2)}, u32[]{:S(2)}) collective-permute-start(f32[4,3,38,134]{3,0,2,1:T(4,128)S(1)} %copy.298), channel_id=1, source_target_pairs={{1,0},{2,1},{3,2},{5,4},{6,5},{7,6},{9,8},{10,9},{11,10},{13,12},{... | collective-permute-start | bytes 733256 | tf_op jit(solution)/shard_map/ppermute | solution.py:29
  33.7 6.9 %collective-permute-start.9 = (f32[8,34,1]{2,1,0:T(8,128)S(1)}, f32[8,34,1]{2,1,0:T(8,128)S(1)}, u32[]{:S(2)}, u32[]{:S(2)}) collective-permute-start(f32[8,34,1]{2,1,0:T(8,128)S(1)} %get-tuple-element.90), channel_id=1, source_target_pairs={{4,0},{8,4},{12,8},{16,12},{20,16},{24,20},{28,24},{5,1},{9,5},{13... | collective-permute-start | bytes 3272 | tf_op jit(solution)/shard_map/ppermute | solution.py:29
  40.8 6.8 %collective-permute-start.10 = (f32[1,34,130]{2,1,0:T(8,128)S(1)}, f32[1,34,130]{2,1,0:T(8,128)S(1)}, u32[]{:S(2)}, u32[]{:S(2)}) collective-permute-start(f32[1,34,130]{2,1,0:T(8,128)S(1)} %get-tuple-element.63), channel_id=1, source_target_pairs={{0,1},{1,2},{2,3},{4,5},{5,6},{6,7},{8,9},{9,10},{10,11},{12,13},{... | collective-permute-start | bytes 53048 | tf_op jit(solution)/shard_map/ppermute | solution.py:28
  44.8 4.7 %collective-permute-start.11 = (f32[1,34,130]{2,1,0:T(8,128)S(1)}, f32[1,34,130]{2,1,0:T(8,128)S(1)}, u32[]{:S(2)}, u32[]{:S(2)}) collective-permute-start(f32[1,34,130]{2,1,0:T(8,128)S(1)} %get-tuple-element.64), channel_id=1, source_target_pairs={{1,0},{2,1},{3,2},{5,4},{6,5},{7,6},{9,8},{10,9},{11,10},{13,12},{... | collective-permute-start | bytes 53048 | tf_op jit(solution)/shard_map/ppermute | solution.py:29
  51.8 5.6 %collective-permute-start.12 = (f32[8,2,128]{2,1,0:T(2,128)S(1)}, f32[8,2,128]{2,1,0:T(2,128)S(1)}, u32[]{:S(2)}, u32[]{:S(2)}) collective-permute-start(f32[8,2,128]{2,1,0:T(2,128)S(1)} %get-tuple-element.101), channel_id=1, source_target_pairs={{0,32},{32,64},{64,96},{96,128},{128,160},{160,192},{192,224},{1,3... | collective-permute-start | bytes 24584 | tf_op jit(solution)/shard_map/ppermute | solution.py:28
  56.0 5.6 %collective-permute-start.13 = (f32[8,2,128]{2,1,0:T(2,128)S(1)}, f32[8,2,128]{2,1,0:T(2,128)S(1)}, u32[]{:S(2)}, u32[]{:S(2)}) collective-permute-start(f32[8,2,128]{2,1,0:T(2,128)S(1)} %get-tuple-element.102), channel_id=1, source_target_pairs={{32,0},{64,32},{96,64},{128,96},{160,128},{192,160},{224,192},{33,... | collective-permute-start | bytes 24584 | tf_op jit(solution)/shard_map/ppermute | solution.py:29
  61.8 6.5 %collective-permute-start.14 = (f32[8,36,2]{2,1,0:T(8,128)S(1)}, f32[8,36,2]{2,1,0:T(8,128)S(1)}, u32[]{:S(2)}, u32[]{:S(2)}) collective-permute-start(f32[8,36,2]{2,1,0:T(8,128)S(1)} %get-tuple-element.87), channel_id=1, source_target_pairs={{0,4},{4,8},{8,12},{12,16},{16,20},{20,24},{24,28},{1,5},{5,9},{9,... | collective-permute-start | bytes 6920 | tf_op jit(solution)/shard_map/ppermute | solution.py:28
  66.0 6.6 %collective-permute-start.15 = (f32[8,36,2]{2,1,0:T(8,128)S(1)}, f32[8,36,2]{2,1,0:T(8,128)S(1)}, u32[]{:S(2)}, u32[]{:S(2)}) collective-permute-start(f32[8,36,2]{2,1,0:T(8,128)S(1)} %get-tuple-element.88), channel_id=1, source_target_pairs={{4,0},{8,4},{12,8},{16,12},{20,16},{24,20},{28,24},{5,1},{9,5},{13... | collective-permute-start | bytes 6920 | tf_op jit(solution)/shard_map/ppermute | solution.py:29
  75.9 5.2 %collective-permute-start.17 = (f32[2,36,132]{2,1,0:T(8,128)S(1)}, f32[2,36,132]{2,1,0:T(8,128)S(1)}, u32[]{:S(2)}, u32[]{:S(2)}) collective-permute-start(f32[2,36,132]{2,1,0:T(8,128)S(1)} %get-tuple-element.56), channel_id=1, source_target_pairs={{1,0},{2,1},{3,2},{5,4},{6,5},{7,6},{9,8},{10,9},{11,10},{13,12},{... | collective-permute-start | bytes 114056 | tf_op jit(solution)/shard_map/ppermute | solution.py:29
  94.1 6.2 %collective-permute-start.19 = (f32[2,36,132]{2,1,0:T(8,128)}, f32[2,36,132]{2,1,0:T(8,128)}, u32[]{:S(2)}, u32[]{:S(2)}) collective-permute-start(f32[2,36,132]{2,1,0:T(8,128)} %get-tuple-element.50), channel_id=1, source_target_pairs={{1,0},{2,1},{3,2},{5,4},{6,5},{7,6},{9,8},{10,9},{11,10},{13,12},{... | collective-permute-start | bytes 114056 | tf_op jit(solution)/shard_map/ppermute | solution.py:29
  101.3 5.7 %collective-permute-start.20 = (f32[8,2,132]{2,0,1:T(8,128)S(1)}, f32[8,2,132]{2,0,1:T(8,128)S(1)}, u32[]{:S(2)}, u32[]{:S(2)}) collective-permute-start(f32[8,2,132]{2,0,1:T(8,128)S(1)} %copy.301), channel_id=1, source_target_pairs={{0,32},{32,64},{64,96},{96,128},{128,160},{160,192},{192,224},{1,3... | collective-permute-start | bytes 25352 | tf_op jit(solution)/shard_map/ppermute | solution.py:28
  107.1 6.0 %collective-permute-start.21 = (f32[8,2,132]{2,0,1:T(8,128)S(1)}, f32[8,2,132]{2,0,1:T(8,128)S(1)}, u32[]{:S(2)}, u32[]{:S(2)}) collective-permute-start(f32[8,2,132]{2,0,1:T(8,128)S(1)} %copy.303), channel_id=1, source_target_pairs={{32,0},{64,32},{96,64},{128,96},{160,128},{192,160},{224,192},{33,... | collective-permute-start | bytes 25352 | tf_op jit(solution)/shard_map/ppermute | solution.py:29
  115.5 9.5 %collective-permute-start.22 = (f32[8,32,2]{2,1,0:T(8,128)}, f32[8,32,2]{2,1,0:T(8,128)}, u32[]{:S(2)}, u32[]{:S(2)}) collective-permute-start(f32[8,32,2]{2,1,0:T(8,128)} %slice.988), channel_id=1, source_target_pairs={{0,4},{4,8},{8,12},{12,16},{16,20},{20,24},{24,28},{1,5},{5,9},{9,... | collective-permute-start | bytes 6152 | tf_op jit(solution)/shard_map/ppermute | solution.py:28
  126.1 7.0 %collective-permute-start.23 = (f32[8,32,2]{2,1,0:T(8,128)S(1)}, f32[8,32,2]{2,1,0:T(8,128)S(1)}, u32[]{:S(2)}, u32[]{:S(2)}) collective-permute-start(f32[8,32,2]{2,1,0:T(8,128)S(1)} %get-tuple-element.76), channel_id=1, source_target_pairs={{4,0},{8,4},{12,8},{16,12},{20,16},{24,20},{28,24},{5,1},{9,5},{13... | collective-permute-start | bytes 6152 | tf_op jit(solution)/shard_map/ppermute | solution.py:29
  134.2 6.2 %collective-permute-start.24 = (f32[8,1,128]{2,1,0:T(1,128)S(1)}, f32[8,1,128]{2,1,0:T(1,128)S(1)}, u32[]{:S(2)}, u32[]{:S(2)}) collective-permute-start(f32[8,1,128]{2,1,0:T(1,128)S(1)} %get-tuple-element.99), channel_id=1, source_target_pairs={{0,32},{32,64},{64,96},{96,128},{128,160},{160,192},{192,224},{1,3... | collective-permute-start | bytes 12296 | tf_op jit(solution)/shard_map/ppermute | solution.py:28
  139.1 4.9 %collective-permute-start.25 = (f32[8,1,128]{2,1,0:T(1,128)S(1)}, f32[8,1,128]{2,1,0:T(1,128)S(1)}, u32[]{:S(2)}, u32[]{:S(2)}) collective-permute-start(f32[8,1,128]{2,1,0:T(1,128)S(1)} %get-tuple-element.100), channel_id=1, source_target_pairs={{32,0},{64,32},{96,64},{128,96},{160,128},{192,160},{224,192},{33,... | collective-permute-start | bytes 12296 | tf_op jit(solution)/shard_map/ppermute | solution.py:29
  144.1 5.3 %collective-permute-start.26 = (f32[8,34,1]{2,1,0:T(8,128)S(1)}, f32[8,34,1]{2,1,0:T(8,128)S(1)}, u32[]{:S(2)}, u32[]{:S(2)}) collective-permute-start(f32[8,34,1]{2,1,0:T(8,128)S(1)} %get-tuple-element.85), channel_id=1, source_target_pairs={{0,4},{4,8},{8,12},{12,16},{16,20},{20,24},{24,28},{1,5},{5,9},{9,... | collective-permute-start | bytes 3272 | tf_op jit(solution)/shard_map/ppermute | solution.py:28
  147.2 6.6 %collective-permute-start.27 = (f32[8,34,1]{2,1,0:T(8,128)S(1)}, f32[8,34,1]{2,1,0:T(8,128)S(1)}, u32[]{:S(2)}, u32[]{:S(2)}) collective-permute-start(f32[8,34,1]{2,1,0:T(8,128)S(1)} %get-tuple-element.86), channel_id=1, source_target_pairs={{4,0},{8,4},{12,8},{16,12},{20,16},{24,20},{28,24},{5,1},{9,5},{13... | collective-permute-start | bytes 3272 | tf_op jit(solution)/shard_map/ppermute | solution.py:29
  153.9 5.0 %collective-permute-start.28 = (f32[1,34,130]{2,1,0:T(8,128)S(1)}, f32[1,34,130]{2,1,0:T(8,128)S(1)}, u32[]{:S(2)}, u32[]{:S(2)}) collective-permute-start(f32[1,34,130]{2,1,0:T(8,128)S(1)} %get-tuple-element.61), channel_id=1, source_target_pairs={{0,1},{1,2},{2,3},{4,5},{5,6},{6,7},{8,9},{9,10},{10,11},{12,13},{... | collective-permute-start | bytes 53048 | tf_op jit(solution)/shard_map/ppermute | solution.py:28
  163.5 6.3 %collective-permute-start.30 = (f32[8,2,128]{2,1,0:T(2,128)S(1)}, f32[8,2,128]{2,1,0:T(2,128)S(1)}, u32[]{:S(2)}, u32[]{:S(2)}) collective-permute-start(f32[8,2,128]{2,1,0:T(2,128)S(1)} %get-tuple-element.97), channel_id=1, source_target_pairs={{0,32},{32,64},{64,96},{96,128},{128,160},{160,192},{192,224},{1,3... | collective-permute-start | bytes 24584 | tf_op jit(solution)/shard_map/ppermute | solution.py:28
  173.1 6.6 %collective-permute-start.32 = (f32[8,36,2]{2,1,0:T(8,128)S(1)}, f32[8,36,2]{2,1,0:T(8,128)S(1)}, u32[]{:S(2)}, u32[]{:S(2)}) collective-permute-start(f32[8,36,2]{2,1,0:T(8,128)S(1)} %get-tuple-element.83), channel_id=1, source_target_pairs={{0,4},{4,8},{8,12},{12,16},{16,20},{20,24},{24,28},{1,5},{5,9},{9,... | collective-permute-start | bytes 6920 | tf_op jit(solution)/shard_map/ppermute | solution.py:28
  177.5 6.6 %collective-permute-start.33 = (f32[8,36,2]{2,1,0:T(8,128)S(1)}, f32[8,36,2]{2,1,0:T(8,128)S(1)}, u32[]{:S(2)}, u32[]{:S(2)}) collective-permute-start(f32[8,36,2]{2,1,0:T(8,128)S(1)} %get-tuple-element.84), channel_id=1, source_target_pairs={{4,0},{8,4},{12,8},{16,12},{20,16},{24,20},{28,24},{5,1},{9,5},{13... | collective-permute-start | bytes 6920 | tf_op jit(solution)/shard_map/ppermute | solution.py:29
  186.2 5.2 %collective-permute-start.35 = (f32[2,36,132]{2,1,0:T(8,128)S(1)}, f32[2,36,132]{2,1,0:T(8,128)S(1)}, u32[]{:S(2)}, u32[]{:S(2)}) collective-permute-start(f32[2,36,132]{2,1,0:T(8,128)S(1)} %get-tuple-element.54), channel_id=1, source_target_pairs={{1,0},{2,1},{3,2},{5,4},{6,5},{7,6},{9,8},{10,9},{11,10},{13,12},{... | collective-permute-start | bytes 114056 | tf_op jit(solution)/shard_map/ppermute | solution.py:29
  196.8 5.6 %collective-permute-start.37 = (f32[2,36,132]{2,1,0:T(8,128)S(1)}, f32[2,36,132]{2,1,0:T(8,128)S(1)}, u32[]{:S(2)}, u32[]{:S(2)}) collective-permute-start(f32[2,36,132]{2,1,0:T(8,128)S(1)} %get-tuple-element.48), channel_id=1, source_target_pairs={{1,0},{2,1},{3,2},{5,4},{6,5},{7,6},{9,8},{10,9},{11,10},{13,12},{... | collective-permute-start | bytes 114056 | tf_op jit(solution)/shard_map/ppermute | solution.py:29
  207.0 4.7 %collective-permute-start.39 = (f32[8,2,132]{2,0,1:T(8,128)S(1)}, f32[8,2,132]{2,0,1:T(8,128)S(1)}, u32[]{:S(2)}, u32[]{:S(2)}) collective-permute-start(f32[8,2,132]{2,0,1:T(8,128)S(1)} %copy.307), channel_id=1, source_target_pairs={{32,0},{64,32},{96,64},{128,96},{160,128},{192,160},{224,192},{33,... | collective-permute-start | bytes 25352 | tf_op jit(solution)/shard_map/ppermute | solution.py:29
  211.9 9.9 %collective-permute-start.40 = (f32[8,32,2]{2,1,0:T(8,128)S(1)}, f32[8,32,2]{2,1,0:T(8,128)S(1)}, u32[]{:S(2)}, u32[]{:S(2)}) collective-permute-start(f32[8,32,2]{2,1,0:T(8,128)S(1)} %slice.1007), channel_id=1, source_target_pairs={{0,4},{4,8},{8,12},{12,16},{16,20},{20,24},{24,28},{1,5},{5,9},{9,... | collective-permute-start | bytes 6152 | tf_op jit(solution)/shard_map/ppermute | solution.py:28
  221.9 7.0 %collective-permute-start.41 = (f32[8,32,2]{2,1,0:T(8,128)S(1)}, f32[8,32,2]{2,1,0:T(8,128)S(1)}, u32[]{:S(2)}, u32[]{:S(2)}) collective-permute-start(f32[8,32,2]{2,1,0:T(8,128)S(1)} %get-tuple-element.74), channel_id=1, source_target_pairs={{4,0},{8,4},{12,8},{16,12},{20,16},{24,20},{28,24},{5,1},{9,5},{13... | collective-permute-start | bytes 6152 | tf_op jit(solution)/shard_map/ppermute | solution.py:29
  229.1 4.9 %collective-permute-start.42 = (f32[8,1,128]{2,1,0:T(1,128)S(1)}, f32[8,1,128]{2,1,0:T(1,128)S(1)}, u32[]{:S(2)}, u32[]{:S(2)}) collective-permute-start(f32[8,1,128]{2,1,0:T(1,128)S(1)} %get-tuple-element.95), channel_id=1, source_target_pairs={{0,32},{32,64},{64,96},{96,128},{128,160},{160,192},{192,224},{1,3... | collective-permute-start | bytes 12296 | tf_op jit(solution)/shard_map/ppermute | solution.py:28
  237.3 5.5 %collective-permute-start.44 = (f32[8,34,1]{2,1,0:T(8,128)S(1)}, f32[8,34,1]{2,1,0:T(8,128)S(1)}, u32[]{:S(2)}, u32[]{:S(2)}) collective-permute-start(f32[8,34,1]{2,1,0:T(8,128)S(1)} %get-tuple-element.81), channel_id=1, source_target_pairs={{0,4},{4,8},{8,12},{12,16},{16,20},{20,24},{24,28},{1,5},{5,9},{9,... | collective-permute-start | bytes 3272 | tf_op jit(solution)/shard_map/ppermute | solution.py:28
  240.5 6.6 %collective-permute-start.45 = (f32[8,34,1]{2,1,0:T(8,128)S(1)}, f32[8,34,1]{2,1,0:T(8,128)S(1)}, u32[]{:S(2)}, u32[]{:S(2)}) collective-permute-start(f32[8,34,1]{2,1,0:T(8,128)S(1)} %get-tuple-element.82), channel_id=1, source_target_pairs={{4,0},{8,4},{12,8},{16,12},{20,16},{24,20},{28,24},{5,1},{9,5},{13... | collective-permute-start | bytes 3272 | tf_op jit(solution)/shard_map/ppermute | solution.py:29
  264.5 6.7 %collective-permute-start.50 = (f32[8,36,2]{2,1,0:T(8,128)S(1)}, f32[8,36,2]{2,1,0:T(8,128)S(1)}, u32[]{:S(2)}, u32[]{:S(2)}) collective-permute-start(f32[8,36,2]{2,1,0:T(8,128)S(1)} %get-tuple-element.79), channel_id=1, source_target_pairs={{0,4},{4,8},{8,12},{12,16},{16,20},{20,24},{24,28},{1,5},{5,9},{9,... | collective-permute-start | bytes 6920 | tf_op jit(solution)/shard_map/ppermute | solution.py:28
  268.9 6.6 %collective-permute-start.51 = (f32[8,36,2]{2,1,0:T(8,128)S(1)}, f32[8,36,2]{2,1,0:T(8,128)S(1)}, u32[]{:S(2)}, u32[]{:S(2)}) collective-permute-start(f32[8,36,2]{2,1,0:T(8,128)S(1)} %get-tuple-element.80), channel_id=1, source_target_pairs={{4,0},{8,4},{12,8},{16,12},{20,16},{24,20},{28,24},{5,1},{9,5},{13... | collective-permute-start | bytes 6920 | tf_op jit(solution)/shard_map/ppermute | solution.py:29
  277.2 5.2 %collective-permute-start.53 = (f32[2,36,132]{2,1,0:T(8,128)S(1)}, f32[2,36,132]{2,1,0:T(8,128)S(1)}, u32[]{:S(2)}, u32[]{:S(2)}) collective-permute-start(f32[2,36,132]{2,1,0:T(8,128)S(1)} %get-tuple-element.52), channel_id=1, source_target_pairs={{1,0},{2,1},{3,2},{5,4},{6,5},{7,6},{9,8},{10,9},{11,10},{13,12},{... | collective-permute-start | bytes 114056 | tf_op jit(solution)/shard_map/ppermute | solution.py:29
  287.9 5.6 %collective-permute-start.55 = (f32[2,36,132]{2,1,0:T(8,128)S(1)}, f32[2,36,132]{2,1,0:T(8,128)S(1)}, u32[]{:S(2)}, u32[]{:S(2)}) collective-permute-start(f32[2,36,132]{2,1,0:T(8,128)S(1)} %get-tuple-element.46), channel_id=1, source_target_pairs={{1,0},{2,1},{3,2},{5,4},{6,5},{7,6},{9,8},{10,9},{11,10},{13,12},{... | collective-permute-start | bytes 114056 | tf_op jit(solution)/shard_map/ppermute | solution.py:29
  298.0 4.7 %collective-permute-start.57 = (f32[8,2,132]{2,0,1:T(8,128)S(1)}, f32[8,2,132]{2,0,1:T(8,128)S(1)}, u32[]{:S(2)}, u32[]{:S(2)}) collective-permute-start(f32[8,2,132]{2,0,1:T(8,128)S(1)} %copy.311), channel_id=1, source_target_pairs={{32,0},{64,32},{96,64},{128,96},{160,128},{192,160},{224,192},{33,... | collective-permute-start | bytes 25352 | tf_op jit(solution)/shard_map/ppermute | solution.py:29
  302.9 9.5 %collective-permute-start.58 = (f32[8,32,2]{2,1,0:T(8,128)S(1)}, f32[8,32,2]{2,1,0:T(8,128)S(1)}, u32[]{:S(2)}, u32[]{:S(2)}) collective-permute-start(f32[8,32,2]{2,1,0:T(8,128)S(1)} %slice.1026), channel_id=1, source_target_pairs={{0,4},{4,8},{8,12},{12,16},{16,20},{20,24},{24,28},{1,5},{5,9},{9,... | collective-permute-start | bytes 6152 | tf_op jit(solution)/shard_map/ppermute | solution.py:28
  312.5 7.0 %collective-permute-start.59 = (f32[8,32,2]{2,1,0:T(8,128)S(1)}, f32[8,32,2]{2,1,0:T(8,128)S(1)}, u32[]{:S(2)}, u32[]{:S(2)}) collective-permute-start(f32[8,32,2]{2,1,0:T(8,128)S(1)} %get-tuple-element.72), channel_id=1, source_target_pairs={{4,0},{8,4},{12,8},{16,12},{20,16},{24,20},{28,24},{5,1},{9,5},{13... | collective-permute-start | bytes 6152 | tf_op jit(solution)/shard_map/ppermute | solution.py:29
  319.7 4.9 %collective-permute-start.60 = (f32[8,1,128]{2,1,0:T(1,128)S(1)}, f32[8,1,128]{2,1,0:T(1,128)S(1)}, u32[]{:S(2)}, u32[]{:S(2)}) collective-permute-start(f32[8,1,128]{2,1,0:T(1,128)S(1)} %get-tuple-element.91), channel_id=1, source_target_pairs={{0,32},{32,64},{64,96},{96,128},{128,160},{160,192},{192,224},{1,3... | collective-permute-start | bytes 12296 | tf_op jit(solution)/shard_map/ppermute | solution.py:28
  327.9 5.5 %collective-permute-start.62 = (f32[8,34,1]{2,1,0:T(8,128)S(1)}, f32[8,34,1]{2,1,0:T(8,128)S(1)}, u32[]{:S(2)}, u32[]{:S(2)}) collective-permute-start(f32[8,34,1]{2,1,0:T(8,128)S(1)} %get-tuple-element.77), channel_id=1, source_target_pairs={{0,4},{4,8},{8,12},{12,16},{16,20},{20,24},{24,28},{1,5},{5,9},{9,... | collective-permute-start | bytes 3272 | tf_op jit(solution)/shard_map/ppermute | solution.py:28
  331.1 6.6 %collective-permute-start.63 = (f32[8,34,1]{2,1,0:T(8,128)S(1)}, f32[8,34,1]{2,1,0:T(8,128)S(1)}, u32[]{:S(2)}, u32[]{:S(2)}) collective-permute-start(f32[8,34,1]{2,1,0:T(8,128)S(1)} %get-tuple-element.78), channel_id=1, source_target_pairs={{4,0},{8,4},{12,8},{16,12},{20,16},{24,20},{28,24},{5,1},{9,5},{13... | collective-permute-start | bytes 3272 | tf_op jit(solution)/shard_map/ppermute | solution.py:29
  337.8 5.0 %collective-permute-start.64 = (f32[1,34,130]{2,1,0:T(8,128)S(1)}, f32[1,34,130]{2,1,0:T(8,128)S(1)}, u32[]{:S(2)}, u32[]{:S(2)}) collective-permute-start(f32[1,34,130]{2,1,0:T(8,128)S(1)} %get-tuple-element.57), channel_id=1, source_target_pairs={{0,1},{1,2},{2,3},{4,5},{5,6},{6,7},{8,9},{9,10},{10,11},{12,13},{... | collective-permute-start | bytes 53048 | tf_op jit(solution)/shard_map/ppermute | solution.py:28
  (35 other events, 649.7 us)
where the time goes:
time: 427 us; the launch traced here: 425 us
  starting transfers between devices  179 us (42%)
  waiting for transfers between devices  131 us (31%)
  blocking collectives  74.4 us (17%)
  other arithmetic  30.3 us (7%)
  local copies, waits for them, and re-layouts  8.6 us (2%)
    ppermute x33, starting transfers between devices, extended(): before = lax.ppermute(last, axis, up)  129 us
    ppermute x33, waiting for transfers between devices, extended(): after = lax.ppermute(leading, axis, down)  116 us
    psum x1, blocking collectives, per_device(): norm_terms.append(lax.psum(local_square, ('gx', 'gy', 'gz')))  74.4 us
    ppermute x33, starting transfers between devices, extended(): after = lax.ppermute(leading, axis, down)  50 us
    ppermute x33, waiting for transfers between devices, extended(): before = lax.ppermute(last, axis, up)  14.6 us
  transfers between devices with their start and end apart: 66, of which 48 were waited for; matrix products, arithmetic and copies ran while one was open for 2% of the time, Pallas kernels for 0%

commit v1 on v0

v1 whole, which is shorter than its diff:
```python
import functools

import jax
import jax.numpy as jnp
from jax import lax
from jax.experimental import pallas as pl
from jax.experimental.pallas import tpu as pltpu
from jax.sharding import PartitionSpec as P

MESH = pl.DeviceIdType.MESH
ITERS = 3
RELAX = 0.9

PLANES, ROWS, LANES, PAD = 14, 40, 128, 8
FLAT = PLANES * ROWS + 2 * PAD
SIDE = ROWS + 2 * PAD
DIRS = tuple(
    (sz, sx, sy)
    for sz in (-1, 0, 1)
    for sx in (-1, 0, 1)
    for sy in (-1, 0, 1)
    if (sz, sx, sy) != (0, 0, 0)
)
DIRS = tuple(sorted(DIRS, key=lambda s: -(abs(s[0]) + abs(s[1]) + abs(s[2]))))
MAIN_DIRS = tuple(s for s in DIRS if s[2] == 0)
SIDE_DIRS = tuple(s for s in DIRS if s[2] != 0)


def plane(z):
    return pl.ds(PAD + ROWS * z, ROWS)


def iota(axis, shape=(ROWS, LANES)):
    return lax.broadcasted_iota(jnp.int32, shape, axis)


def roll(x, shift):
    return pltpu.roll(x, shift % LANES, axis=x.ndim - 1)


def row_tile(sx):
    return {0: pl.ds(0, ROWS), 1: pl.ds(ROWS - 8, 8), -1: pl.ds(0, 8)}[sx]


def add_tiles(acc, first, last):
    return jnp.concatenate([acc[:8] + first, acc[8 : ROWS - 8], acc[ROWS - 8 :] + last], axis=0)


def kernel(
    sizes, src_hbm, perm_hbm, stor_hbm, depth_hbm, out_hbm, hist_ref,
    in_src, in_perm, in_stor, in_depth, out_buf,
    own, own_side, own_corner,
    rz_k, rz_s, rz_q, rx0, rzx0, ry0, rxy0, rzy0, rzxy0,
    send, send_side, rz, rx, rzx, ry, rxy,
    k_main, k_side, s_main, s_side,
    w_main, w_side, alpha, alpha_side, scale,
    r0_main, r0_side, r_main, r_side, a_main, a_side, b_main, b_side, p_main, p_side,
    part, part_in,
    load_sem, out_sem, send0, recv0, sends, recvs, ar_send, ar_recv,
):
    n_gx, n_gy, n_gz = sizes
    gx, gy, gz = lax.axis_index("gx"), lax.axis_index("gy"), lax.axis_index("gz")

    def device(s):
        return (
            lax.rem(gx + s[1] + n_gx, n_gx),
            lax.rem(gy + s[2] + n_gy, n_gy),
            lax.rem(gz + s[0] + n_gz, n_gz),
        )

    barrier = pltpu.get_barrier_semaphore()
    for s in DIRS:
        pl.semaphore_signal(barrier, inc=1, device_id=device(s), device_id_type=MESH)

    loads = [
        pltpu.make_async_copy(a, b, load_sem.at[i])
        for i, (a, b) in enumerate(
            ((depth_hbm, in_depth), (perm_hbm, in_perm), (stor_hbm, in_stor), (src_hbm, in_src))
        )
    ]
    for copy in loads:
        copy.start()

    zero_plane = jnp.zeros((ROWS, LANES), jnp.float32)
    own[...] = jnp.zeros(own.shape, jnp.float32)
    for ref in (k_main, s_main, r0_main, r_main, a_main, b_main, p_main):
        ref[0 : PAD + ROWS] = jnp.zeros((PAD + ROWS, LANES), jnp.float32)
        ref[FLAT - PAD - ROWS :] = jnp.zeros((PAD + ROWS, LANES), jnp.float32)
    for ref in (k_side, s_side, r0_side, r_side, a_side, b_side, p_side):
        ref[...] = jnp.zeros((SIDE, LANES), jnp.float32)

    lane = iota(1)
    row = iota(0)
    group = lane // 8
    j = lane % 8
    left = jnp.logical_and(j >= 4, j <= 6)
    right = jnp.logical_and(j >= 1, j <= 3)

    def gather_edges(acc, z, value):
        return jnp.where(group == z, roll(value, 8 * z + 4), acc)

    for copy in loads:
        copy.wait()

    depth = in_depth[...]
    edges = [zero_plane, zero_plane, zero_plane]
    for z in range(8):
        active = (gz * 8 + z) < depth
        for f, value in enumerate(
            (jnp.where(active, in_perm[z], 0.0), in_stor[z], in_src[z])
        ):
            own[f, z + 3, 4:36] = value
            edges[f] = gather_edges(edges[f], z + 3, own[f, z + 3])
    sides = []
    for f in range(3):
        to_right = jnp.where(left, roll(edges[f], 3), 0.0)
        to_left = jnp.where(right, roll(edges[f], -3), 0.0)
        own_side[0, f] = to_left
        own_side[1, f] = to_right
        sides.append((to_left, to_right))
    for d in range(2):
        for u, base in ((0, 24), (1, 64)):
            k, st, q = (sides[f][d] for f in range(3))
            moved_s, moved_q = roll(st, 24), roll(q, 48)
            in_k = jnp.logical_and(lane >= base, lane < base + 24)
            in_s = jnp.logical_and(lane >= base + 24, lane < base + 48)
            own_corner[u, d] = jnp.where(in_k, k, jnp.where(in_s, moved_s, moved_q))

    pl.semaphore_wait(barrier, len(DIRS))

    started = []
    exchange0 = []

    def post0(src, dst, s):
        i = len(exchange0)
        copy = pltpu.make_async_remote_copy(
            src_ref=src, dst_ref=dst, send_sem=send0.at[i], recv_sem=recv0.at[i],
            device_id=device(s), device_id_type=MESH,
        )
        copy.start()
        exchange0.append(copy)
        started.append(copy)

    side_of = lambda v: (v + 1) // 2
    for s in DIRS:
        sz, sx, sy = s
        u, v, d = side_of(sz), side_of(sx), side_of(sy)
        if sy == 0:
            if sz == 0:
                post0(own.at[:, pl.ds(3, 8), row_tile(sx)], rx0.at[v], s)
            elif sx == 0:
                post0(own.at[0, pl.ds(8 if sz > 0 else 3, 3)], rz_k.at[u], s)
                post0(own.at[1, pl.ds(9 if sz > 0 else 3, 2)], rz_s.at[u], s)
                post0(own.at[2, pl.ds(9 if sz > 0 else 3, 2)], rz_q.at[u], s)
            else:
                post0(own.at[:, pl.ds(8 if sz > 0 else 3, 3), row_tile(sx)], rzx0.at[u, v], s)
        elif sz == 0:
            if sx == 0:
                post0(own_side.at[d], ry0.at[d], s)
            else:
                post0(own_side.at[d, :, row_tile(sx)], rxy0.at[v, d], s)
        elif sx == 0:
            post0(own_corner.at[u, d], rzy0.at[u, d], s)
        else:
            post0(own_corner.at[u, d, row_tile(sx)], rzxy0.at[u, v, d], s)
    for copy in exchange0:
        copy.wait_recv()

    x = row - 4
    row_in = jnp.logical_and(
        jnp.logical_or(x >= 0, gx > 0), jnp.logical_or(x < 32, gx < n_gx - 1)
    )
    side_in = jnp.logical_or(
        jnp.logical_and(left, gy > 0), jnp.logical_and(right, gy < n_gy - 1)
    )
    group_in = jnp.logical_and(
        jnp.logical_or(group >= 3, gz > 0), jnp.logical_or(group < 11, gz < n_gz - 1)
    )
    side_in = jnp.logical_and(jnp.logical_and(side_in, group_in), row_in)

    def plane_in(z):
        if z < 3:
            return (gz > 0).astype(jnp.float32)
        if z > 10:
            return (gz < n_gz - 1).astype(jnp.float32)
        return jnp.float32(1.0)

    def first_main(f, z, rz_f, low):
        if 3 <= z <= 10:
            value = own[f, z]
            return add_tiles(value, rx0[1, f, z - 3], rx0[0, f, z - 3])
        if z < 3:
            value = rz_f[1, z - low] if z >= low else zero_plane
            return add_tiles(value, rzx0[1, 1, f, z], rzx0[1, 0, f, z])
        value = rz_f[0, z - 11] if z - 11 < 3 - low else zero_plane
        return add_tiles(value, rzx0[0, 1, f, z - 11], rzx0[0, 0, f, z - 11])

    def first_side(f):
        total = []
        for d in range(2):
            shift = 64 - 24 * f

            def corner(lower, upper):
                g = lax.broadcasted_iota(jnp.int32, lower.shape, 1) // 8
                return jnp.where(
                    g <= 2, roll(lower, shift),
                    jnp.where(jnp.logical_and(g >= 11, g <= 13), roll(upper, shift), 0.0),
                )

            value = ry0[d, f] + corner(rzy0[1, d], rzy0[0, d])
            first, last = (
                rxy0[v, d, f] + corner(rzxy0[1, v, d], rzxy0[0, v, d]) for v in (1, 0)
            )
            total.append(add_tiles(value, first, last))
        return jnp.where(left, total[1], 0.0) + jnp.where(right, total[0], 0.0)

    row_gain = row_in.astype(jnp.float32)
    k_edges = zero_plane
    for z in range(PLANES):
        value = first_main(0, z, rz_k, 0) * (row_gain * plane_in(z))
        k_main[plane(z)] = value
        k_edges = gather_edges(k_edges, z, value)
    k_side[pl.ds(PAD, ROWS)] = jnp.where(side_in, first_side(0), 0.0)

    def to_main(side):
        return jnp.where(j == 4, roll(side, -2), roll(side, 2))

    def main_neighbours(ref, z, centre, cross):
        base = PAD + ROWS * z
        moved = roll(cross, -(8 * z + 4))
        return (
            ref[pl.ds(base - ROWS, ROWS)],
            ref[pl.ds(base + ROWS, ROWS)],
            ref[pl.ds(base - 1, ROWS)],
            ref[pl.ds(base + 1, ROWS)],
            jnp.where(lane == 0, moved, roll(centre, 1)),
            jnp.where(lane == LANES - 1, moved, roll(centre, -1)),
        )

    def side_neighbours(ref, centre, edges):
        return (
            roll(centre, 8),
            roll(centre, -8),
            ref[pl.ds(PAD - 1, ROWS)],
            ref[pl.ds(PAD + 1, ROWS)],
            jnp.where(j == 1, roll(edges, -2), roll(centre, 1)),
            jnp.where(j == 6, roll(edges, 2), roll(centre, -1)),
        )

    def weights(centre, others, storage, source, keep):
        idle = jnp.where(centre > 0.0, 0.0, 1.0)
        diagonal = storage + idle
        couplings = []
        for other in others:
            other_idle = jnp.where(other > 0.0, 0.0, 1.0)
            c = (2.0 * centre) * other / ((centre + idle) + (other + other_idle))
            couplings.append(c)
            diagonal = diagonal + c
        gain = jnp.where(keep, RELAX / diagonal, 0.0)
        live = jnp.where(keep, 1.0 - idle, 0.0)
        return [c * gain for c in couplings], live * gain * source, live * RELAX, diagonal

    rows_kept = jnp.logical_and(row >= 2, row < 38)
    rows_own = jnp.logical_and(row >= 4, row < 36)
    cross = to_main(k_side[pl.ds(PAD, ROWS)])
    edges = zero_plane
    total = zero_plane
    for z in range(1, 13):
        centre = k_main[plane(z)]
        ws, r, al, diagonal = weights(
            centre, main_neighbours(k_main, z, centre, cross),
            first_main(1, z, rz_s, 1), first_main(2, z, rz_q, 1), rows_kept,
        )
        for i in range(6):
            w_main[i, z - 1] = ws[i]
        alpha[z - 1] = al
        r0_main[plane(z)] = r
        edges = gather_edges(edges, z, r)
        if 3 <= z <= 10:
            sc = jnp.where(rows_own, diagonal * (1.0 / RELAX), 0.0)
            scale[z - 3] = sc
            total = total + (r * sc) * (r * sc)
    side_kept = jnp.logical_and(
        jnp.logical_and(rows_kept, jnp.logical_and(group >= 1, group <= 12)),
        jnp.logical_or(jnp.logical_or(j == 1, j == 2), jnp.logical_or(j == 5, j == 6)),
    )
    centre = k_side[pl.ds(PAD, ROWS)]
    ws, r, al, _ = weights(
        centre, side_neighbours(k_side, centre, k_edges), first_side(1), first_side(2), side_kept
    )
    for i in range(6):
        w_side[i] = ws[i]
    alpha_side[...] = al
    r0_side[pl.ds(PAD, ROWS)] = r

    def half(flag):
        return jnp.where(flag, 0.5, 1.0)

    def axis_gain(position, extent, owner, owners):
        inner_low = jnp.logical_and(jnp.logical_and(position >= 0, position < 2), owner > 0)
        inner_high = jnp.logical_and(
            jnp.logical_and(position >= extent - 2, position < extent), owner < owners - 1
        )
        outer = jnp.logical_or(
            jnp.logical_and(position >= -2, position < 0),
            jnp.logical_and(position >= extent, position < extent + 2),
        )
        return half(jnp.logical_or(outer, jnp.logical_or(inner_low, inner_high)))

    x_gain = axis_gain(x, 32, gx, n_gx)
    main_gain = x_gain * axis_gain(lane, 128, gy, n_gy)
    side_gain = (
        x_gain * axis_gain(group - 3, 8, gz, n_gz)
        * half(jnp.logical_or(jnp.logical_or(j == 1, j == 2), jnp.logical_or(j == 5, j == 6)))
    )

    def z_gain(z):
        if z in (0, 13):
            return 1.0
        if z in (1, 2, 11, 12):
            return 0.5
        if z in (3, 4):
            return jnp.where(gz > 0, 0.5, 1.0)
        if z in (9, 10):
            return jnp.where(gz < n_gz - 1, 0.5, 1.0)
        return 1.0

    def sweep(src, src_side, edges, rhs, rhs_side, write_main, write_side):
        side = src_side[pl.ds(PAD, ROWS)]
        value = (1.0 - RELAX) * side + rhs_side[pl.ds(PAD, ROWS)]
        for i, other in enumerate(side_neighbours(src_side, side, edges)):
            value = value + w_side[i] * other
        write_side(value)
        cross = to_main(side)
        new_edges = zero_plane
        for z in range(1, 13):
            centre = src[plane(z)]
            value = (1.0 - RELAX) * centre + rhs[plane(z)]
            for i, other in enumerate(main_neighbours(src, z, centre, cross)):
                value = value + w_main[i, z - 1] * other
            write_main(z, value)
            new_edges = gather_edges(new_edges, z, value)
        return new_edges

    def into(ref):
        def write(z, value):
            ref[plane(z)] = value
        return write

    def into_side(ref):
        def write(value):
            ref[pl.ds(PAD, ROWS)] = value
        return write

    partials = [total]
    for k in range(ITERS):
        rhs, rhs_side = (r0_main, r0_side) if k == 0 else (r_main, r_side)
        edges = sweep(rhs, rhs_side, edges, rhs, rhs_side, into(a_main), into_side(a_side))
        edges = sweep(a_main, a_side, edges, rhs, rhs_side, into(b_main), into_side(b_side))

        def last_main(z, value):
            send[k, z] = value

        def last_side(value):
            send[k, 0] = value
            send[k, 13] = value

        edges = sweep(b_main, b_side, edges, rhs, rhs_side, last_main, last_side)
        side = send[k, 0]
        send_side[k, 1] = jnp.where(
            left, roll(edges, 3), jnp.where(jnp.logical_or(j == 1, j == 2), side, 0.0)
        )
        send_side[k, 0] = jnp.where(
            right, roll(edges, -3), jnp.where(jnp.logical_or(j == 5, j == 6), side, 0.0)
        )

        copies = []
        for i, s in enumerate(DIRS):
            sz, sx, sy = s
            u, v, d = side_of(sz), side_of(sx), side_of(sy)
            if sy == 0:
                planes = {0: pl.ds(0, 13), 1: pl.ds(8, 6), -1: pl.ds(0, 6)}[sz]
                source = send.at[k, planes, row_tile(sx)]
                if sz == 0:
                    target = rx.at[k, v]
                elif sx == 0:
                    target = rz.at[k, u]
                else:
                    target = rzx.at[k, u, v]
            else:
                source = send_side.at[k, d, row_tile(sx)]
                target = ry.at[k, sz + 1, d] if sx == 0 else rxy.at[k, sz + 1, v, d]
            copy = pltpu.make_async_remote_copy(
                src_ref=source, dst_ref=target, send_sem=sends.at[k, i], recv_sem=recvs.at[k, i],
                device_id=device(s), device_id_type=MESH,
            )
            copy.start()
            copies.append(copy)
            started.append(copy)
        for copy in copies:
            copy.wait_recv()

        def across(lower, upper):
            at = lax.broadcasted_iota(jnp.int32, lower.shape, 1)
            return roll(jnp.where(at >= 64, lower, jnp.where(at < 48, upper, 0.0)), 64)

        side_sum = add_tiles(
            side + across(rz[k, 1, 5], rz[k, 0, 0]),
            rx[k, 1, 0] + across(rzx[k, 1, 1, 5], rzx[k, 0, 1, 0]),
            rx[k, 0, 0] + across(rzx[k, 1, 0, 5], rzx[k, 0, 0, 0]),
        )
        beside = [
            add_tiles(
                ry[k, 1, d] + across(ry[k, 2, d], ry[k, 0, d]),
                rxy[k, 1, 1, d] + across(rxy[k, 2, 1, d], rxy[k, 0, 1, d]),
                rxy[k, 1, 0, d] + across(rxy[k, 2, 0, d], rxy[k, 0, 0, d]),
            )
            for d in range(2)
        ]
        side_sum = side_sum + jnp.where(left, beside[1], 0.0) + jnp.where(right, beside[0], 0.0)
        inward = jnp.where(
            jnp.logical_or(j == 4, j == 5), roll(beside[1], 3), roll(beside[0], -3)
        )
        outermost = jnp.logical_or(lane < 2, lane >= LANES - 2)
        new_side = p_side[pl.ds(PAD, ROWS)] + side_sum * side_gain
        p_side[pl.ds(PAD, ROWS)] = new_side
        p_edges = zero_plane
        for z in range(PLANES):
            value = send[k, z] if 1 <= z <= 12 else zero_plane
            first = rx[k, 1, z] if 1 <= z <= 12 else jnp.zeros((8, LANES), jnp.float32)
            last = rx[k, 0, z] if 1 <= z <= 12 else jnp.zeros((8, LANES), jnp.float32)
            if z <= 4:
                value = value + rz[k, 1, z]
                first = first + rzx[k, 1, 1, z]
                last = last + rzx[k, 1, 0, z]
            if z >= 9:
                value = value + rz[k, 0, z - 8]
                first = first + rzx[k, 0, 1, z - 8]
                last = last + rzx[k, 0, 0, z - 8]
            value = add_tiles(value, first, last)
            value = value + jnp.where(outermost, roll(inward, -(8 * z + 4)), 0.0)
            value = value * (main_gain * z_gain(z))
            if k > 0:
                value = p_main[plane(z)] + value
            p_main[plane(z)] = value
            p_edges = gather_edges(p_edges, z, value)

        cross = to_main(new_side)
        edges = zero_plane
        total = zero_plane
        last_one = k == ITERS - 1
        for z in range(3, 11) if last_one else range(1, 13):
            centre = p_main[plane(z)]
            value = r0_main[plane(z)] - alpha[z - 1] * centre
            for i, other in enumerate(main_neighbours(p_main, z, centre, cross)):
                value = value + w_main[i, z - 1] * other
            if not last_one:
                r_main[plane(z)] = value
                edges = gather_edges(edges, z, value)
            if 3 <= z <= 10:
                value = value * scale[z - 3]
                total = total + value * value
        if not last_one:
            value = r0_side[pl.ds(PAD, ROWS)] - alpha_side[...] * new_side
            for i, other in enumerate(side_neighbours(p_side, new_side, p_edges)):
                value = value + w_side[i] * other
            r_side[pl.ds(PAD, ROWS)] = value
        partials.append(total)

    for z in range(8):
        out_buf[z] = p_main[pl.ds(PAD + ROWS * (z + 3) + 4, 32)]
    out_copy = pltpu.make_async_copy(out_buf, out_hbm, out_sem)
    out_copy.start()

    row8 = iota(0, (8, LANES))
    mine = jnp.zeros((8, LANES), jnp.float32)
    for i, value in enumerate(partials):
        mine = jnp.where(row8 == i, jnp.sum(value, axis=0, keepdims=True), mine)
    pair = gy + 1 - 2 * lax.rem(gy, 2)
    rounds = (
        [
            (lax.rem(gx + i, n_gx), gy if h == 0 else pair, gz)
            for i in range(n_gx)
            for h in range(2)
            if (i, h) != (0, 0)
        ],
        [
            (gx, lax.rem(gy + 2 * i, n_gy), lax.rem(gz + h, n_gz))
            for i in range(n_gy // 2)
            for h in range(n_gz)
            if (i, h) != (0, 0)
        ],
    )
    for n, targets in enumerate(rounds):
        part[n] = mine
        copies = []
        for i, target in enumerate(targets):
            copy = pltpu.make_async_remote_copy(
                src_ref=part.at[n], dst_ref=part_in.at[n, i],
                send_sem=ar_send.at[n, i], recv_sem=ar_recv.at[n, i],
                device_id=target, device_id_type=MESH,
            )
            copy.start()
            copies.append(copy)
            started.append(copy)
        for copy in copies:
            copy.wait_recv()
        terms = [mine] + [part_in[n, i] for i in range(len(targets))]
        while len(terms) > 1:
            terms = [sum(terms[i : i + 2]) for i in range(0, len(terms), 2)]
        mine = terms[0]
    squares = jnp.sum(mine, axis=1, keepdims=True)
    ratio = jnp.sqrt(squares / squares[0:1])
    for i in range(ITERS):
        hist_ref[i] = jnp.sum(ratio[i + 1 : i + 2, :])
    out_copy.wait()
    for copy in started:
        copy.wait_send()


def solution(mesh):
    sizes = (mesh.shape["gx"], mesh.shape["gy"], mesh.shape["gz"])
    f32 = jnp.float32

    def vmem(*shape):
        return pltpu.VMEM(shape, f32)

    n_dirs = len(DIRS)
    n_first = n_dirs + 4
    scratch = [
        vmem(8, 32, LANES), vmem(8, 32, LANES), vmem(8, 32, LANES),
        pltpu.VMEM((32, LANES), jnp.int32), vmem(8, 32, LANES),
        vmem(3, PLANES, ROWS, LANES), vmem(2, 3, ROWS, LANES), vmem(2, 2, ROWS, LANES),
        vmem(2, 3, ROWS, LANES), vmem(2, 2, ROWS, LANES), vmem(2, 2, ROWS, LANES),
        vmem(2, 3, 8, 8, LANES), vmem(2, 2, 3, 3, 8, LANES),
        vmem(2, 3, ROWS, LANES), vmem(2, 2, 3, 8, LANES),
        vmem(2, 2, ROWS, LANES), vmem(2, 2, 2, 8, LANES),
        vmem(ITERS, PLANES, ROWS, LANES), vmem(ITERS, 2, ROWS, LANES),
        vmem(ITERS, 2, 6, ROWS, LANES), vmem(ITERS, 2, 13, 8, LANES),
        vmem(ITERS, 2, 2, 6, 8, LANES),
        vmem(ITERS, 3, 2, ROWS, LANES), vmem(ITERS, 3, 2, 2, 8, LANES),
        vmem(FLAT, LANES), vmem(SIDE, LANES), vmem(FLAT, LANES), vmem(SIDE, LANES),
        vmem(6, 12, ROWS, LANES), vmem(6, ROWS, LANES),
        vmem(12, ROWS, LANES), vmem(ROWS, LANES), vmem(8, ROWS, LANES),
    ]
    for _ in range(5):
        scratch += [vmem(FLAT, LANES), vmem(SIDE, LANES)]
    scratch += [
        vmem(2, 8, LANES), vmem(2, 15, 8, LANES),
        pltpu.SemaphoreType.DMA((4,)), pltpu.SemaphoreType.DMA,
        pltpu.SemaphoreType.DMA((n_first,)), pltpu.SemaphoreType.DMA((n_first,)),
        pltpu.SemaphoreType.DMA((ITERS, n_dirs)), pltpu.SemaphoreType.DMA((ITERS, n_dirs)),
        pltpu.SemaphoreType.DMA((2, 15)), pltpu.SemaphoreType.DMA((2, 15)),
    ]

    def per_device(source, permeability, storage, column_depth):
        return pl.pallas_call(
            functools.partial(kernel, sizes),
            out_shape=(
                jax.ShapeDtypeStruct(source.shape, f32),
                jax.ShapeDtypeStruct((ITERS,), f32),
            ),
            in_specs=[pl.BlockSpec(memory_space=pl.ANY)] * 4,
            out_specs=(
                pl.BlockSpec(memory_space=pl.ANY),
                pl.BlockSpec(memory_space=pltpu.SMEM),
            ),
            scratch_shapes=scratch,
            compiler_params=pltpu.CompilerParams(
                collective_id=0, has_side_effects=True, vmem_limit_bytes=40 * 2**20
            ),
            name="schwarz",
        )(source, permeability, storage, column_depth)

    placed = (P("gz", "gx", "gy"), P("gz", "gx", "gy"), P("gz", "gx", "gy"), P("gx", "gy"))
    return jax.shard_map(
        per_device,
        mesh=mesh,
        in_specs=placed,
        out_specs=(P("gz", "gx", "gy"), P()),
        check_vma=False,
    )
```

time: 427 us -> 70.8 us (0.17)
  starting transfers between devices: 179 us -> 0 us
  waiting for transfers between devices: 131 us -> 0 us
  blocking collectives: 74.4 us -> 0 us
  Pallas kernels: 0 us -> 65.3 us
  other arithmetic: 30.3 us -> 0 us
    ppermute x66 -> x0, starting transfers between devices: 179 us -> none  [the longest x33 129 us: extended(): before = lax.ppermute(last, axis, up)]
    ppermute x66 -> x0, waiting for transfers between devices: 131 us -> none  [the longest x33 116 us: extended(): after = lax.ppermute(leading, axis, down)]
    psum x1 -> x0, blocking collectives: 74.4 us -> none  [per_device(): norm_terms.append(lax.psum(local_square, ('gx', 'gy', 'gz')))]
    pallas_call x0 -> x1, Pallas kernels: none -> 65.3 us  [per_device(): pl.pallas_call(functools.partial(kernel, sizes), out_shape=(jax.ShapeDtyp...]
    add x33 -> x0, other arithmetic: 11.3 us -> none  [the longest x9 5.97 us: local_solve(): correction + RELAXATION * (residual_block - apply_operator(widened, coupl...]
    slice x41 -> x0, local copies, waits for them, and re-layouts: 7.05 us -> none  [the longest x9 2.76 us: edge_layers(): lax.slice_in_dim(field, extent - 2, extent, axis=axis_dim)]
    reduce_sum x4 -> x0, other arithmetic: 5.2 us -> none  [per_device(): local_square = jnp.sum(residual * residual)]
    unnamed x36 -> x10, local copies, waits for them, and re-layouts: 0.09 us -> 4.59 us
  transfers between devices with their start and end apart: 66 -> 0, of which waited for: 48 -> 0; matrix products, arithmetic and copies ran while one was open for 2% -> 0% of each run, Pallas kernels for 0% -> 0%
where the time goes in v1:
time: 70.8 us; the launch traced here: 70.6 us
  Pallas kernels  65.3 us (92%)
  local copies, waits for them, and re-layouts  4.59 us (6%)
    pallas_call x1, Pallas kernels, per_device(): pl.pallas_call(functools.partial(kernel, sizes), out_shape=(jax.ShapeDtyp...  65.3 us
    unnamed x10, local copies, waits for them, and re-layouts  4.59 us

profile of v1, /device:TPU:1, one launch (start us, length us, event | category | flops | bytes accessed | tf_op | source)
XLA Modules:
  0.0 70.6 jit_solution(17411793042947488072)
XLA Ops:
  0.6 0.0 copy-start
  0.6 0.9 %copy-done = f32[8,32,128]{2,1,0:T(8,128)S(1)} copy-done((f32[8,32,128]{2,1,0:T(8,128)S(1)}, f32[8,32,128]{2,1,0:T(8,128)}, u32[]{:S(2)}) %copy-start) | copy-done | bytes 131096
  1.5 0.0 copy-start.1
  1.5 0.9 %copy-done.1 = f32[8,32,128]{2,1,0:T(8,128)S(1)} copy-done((f32[8,32,128]{2,1,0:T(8,128)S(1)}, f32[8,32,128]{2,1,0:T(8,128)}, u32[]{:S(2)}) %copy-start.1) | copy-done | bytes 131096
  2.4 0.0 copy-start.2
  2.4 0.9 %copy-done.2 = f32[8,32,128]{2,1,0:T(8,128)S(1)} copy-done((f32[8,32,128]{2,1,0:T(8,128)S(1)}, f32[8,32,128]{2,1,0:T(8,128)}, u32[]{:S(2)}) %copy-start.2) | copy-done | bytes 131096
  3.3 0.0 copy-start.3
  3.3 0.7 %copy-done.3 = s32[32,128]{1,0:T(8,128)S(1)} copy-done((s32[32,128]{1,0:T(8,128)S(1)}, s32[32,128]{1,0:T(8,128)}, u32[]{:S(2)}) %copy-start.3) | copy-done | bytes 16408
  4.1 65.3 %schwarz.1 = (f32[8,32,128]{2,1,0:T(8,128)S(1)}, f32[3]{0:T(128)S(1)}) custom-call(f32[8,32,128]{2,1,0:T(8,128)S(1)} %copy-done, f32[8,32,128]{2,1,0:T(8,128)S(1)} %copy-done.1, f32[8,32,128]{2,1,0:T(8,128)S(1)} %copy-done.2, s32[32,128]{1,0:T(8,128)S(1)} %copy-done.3), custom_call_target="tpu_custom_call" | custom-call | tf_op jit(solution)/shard_map/schwarz/pallas_call | solution.py:557
  69.4 0.7 copy.8
  70.1 0.5 copy.9
Async XLA Ops:
  0.6 0.9 %copy-start = (f32[8,32,128]{2,1,0:T(8,128)S(1)}, f32[8,32,128]{2,1,0:T(8,128)}, u32[]{:S(2)}) copy-start(f32[8,32,128]{2,1,0:T(8,128)} %src_hbm.1) | copy-start | bytes 393220
  1.5 0.9 %copy-start.1 = (f32[8,32,128]{2,1,0:T(8,128)S(1)}, f32[8,32,128]{2,1,0:T(8,128)}, u32[]{:S(2)}) copy-start(f32[8,32,128]{2,1,0:T(8,128)} %perm_hbm.1) | copy-start | bytes 393220
  2.4 0.9 %copy-start.2 = (f32[8,32,128]{2,1,0:T(8,128)S(1)}, f32[8,32,128]{2,1,0:T(8,128)}, u32[]{:S(2)}) copy-start(f32[8,32,128]{2,1,0:T(8,128)} %stor_hbm.1) | copy-start | bytes 393220
  3.3 0.7 %copy-start.3 = (s32[32,128]{1,0:T(8,128)S(1)}, s32[32,128]{1,0:T(8,128)}, u32[]{:S(2)}) copy-start(s32[32,128]{1,0:T(8,128)} %depth_hbm.1) | copy-start | bytes 49156

commit v2 on v1

--- a/solution.py
+++ b/solution.py
@@ -472,47 +472,57 @@
     out_copy = pltpu.make_async_copy(out_buf, out_hbm, out_sem)
     out_copy.start()
 
-    row8 = iota(0, (8, LANES))
-    mine = jnp.zeros((8, LANES), jnp.float32)
+    at = iota(1, (1, LANES)) // 32
+    mine = jnp.zeros((1, LANES), jnp.float32)
     for i, value in enumerate(partials):
-        mine = jnp.where(row8 == i, jnp.sum(value, axis=0, keepdims=True), mine)
+        value = jnp.sum(value, axis=0, keepdims=True)
+        value = value + roll(value, 64)
+        mine = jnp.where(at == i, value + roll(value, 32), mine)
     pair = gy + 1 - 2 * lax.rem(gy, 2)
+
+    def ring(i, n):
+        return min(i, n - i)
+
     rounds = (
-        [
-            (lax.rem(gx + i, n_gx), gy if h == 0 else pair, gz)
-            for i in range(n_gx)
-            for h in range(2)
-            if (i, h) != (0, 0)
-        ],
-        [
-            (gx, lax.rem(gy + 2 * i, n_gy), lax.rem(gz + h, n_gz))
-            for i in range(n_gy // 2)
-            for h in range(n_gz)
-            if (i, h) != (0, 0)
-        ],
-    )
+        sorted(
+            ((i, h) for i in range(n_gx) for h in range(2) if (i, h) != (0, 0)),
+            key=lambda t: -ring(t[0], n_gx) - 0.3 * t[1],
+        ),
+        sorted(
+            ((i, h) for i in range(n_gy // 2) for h in range(n_gz) if (i, h) != (0, 0)),
+            key=lambda t: -ring(t[0], n_gy // 2) - ring(t[1], n_gz),
+        ),
+    )
+    rounds = (
+        [(lax.rem(gx + i, n_gx), gy if h == 0 else pair, gz) for i, h in rounds[0]],
+        [(gx, lax.rem(gy + 2 * i, n_gy), lax.rem(gz + h, n_gz)) for i, h in rounds[1]],
+    )
+    slots = (gx * 2 + lax.rem(gy, 2), (gy // 2) * n_gz + gz)
     for n, targets in enumerate(rounds):
-        part[n] = mine
+        here = part_in.at[n, slots[n], pl.ds(0, 1)]
+        part[n, 0:1] = mine
         copies = []
         for i, target in enumerate(targets):
             copy = pltpu.make_async_remote_copy(
-                src_ref=part.at[n], dst_ref=part_in.at[n, i],
+                src_ref=part.at[n, pl.ds(0, 1)], dst_ref=here,
                 send_sem=ar_send.at[n, i], recv_sem=ar_recv.at[n, i],
                 device_id=target, device_id_type=MESH,
             )
             copy.start()
             copies.append(copy)
             started.append(copy)
+        here[...] = mine
         for copy in copies:
             copy.wait_recv()
-        terms = [mine] + [part_in[n, i] for i in range(len(targets))]
+        terms = [part_in[n, i, 0:1] for i in range(len(targets) + 1)]
         while len(terms) > 1:
-            terms = [sum(terms[i : i + 2]) for i in range(0, len(terms), 2)]
+            terms = [sum(terms[i + 1 : i + 2], terms[i]) for i in range(0, len(terms), 2)]
         mine = terms[0]
-    squares = jnp.sum(mine, axis=1, keepdims=True)
-    ratio = jnp.sqrt(squares / squares[0:1])
+    squares = [
+        jnp.sum(jnp.where(at == i, mine, 0.0), axis=1, keepdims=True) for i in range(ITERS + 1)
+    ]
     for i in range(ITERS):
-        hist_ref[i] = jnp.sum(ratio[i + 1 : i + 2, :])
+        hist_ref[i] = jnp.sum(jnp.sqrt(squares[i + 1] / squares[0]))
     out_copy.wait()
     for copy in started:
         copy.wait_send()
@@ -546,7 +556,7 @@
     for _ in range(5):
         scratch += [vmem(FLAT, LANES), vmem(SIDE, LANES)]
     scratch += [
-        vmem(2, 8, LANES), vmem(2, 15, 8, LANES),
+        vmem(2, 8, LANES), vmem(2, 16, 8, LANES),
         pltpu.SemaphoreType.DMA((4,)), pltpu.SemaphoreType.DMA,
         pltpu.SemaphoreType.DMA((n_first,)), pltpu.SemaphoreType.DMA((n_first,)),
         pltpu.SemaphoreType.DMA((ITERS, n_dirs)), pltpu.SemaphoreType.DMA((ITERS, n_dirs)),
@@ -567,7 +577,7 @@
             ),
             scratch_shapes=scratch,
             compiler_params=pltpu.CompilerParams(
-                collective_id=0, has_side_effects=True, vmem_limit_bytes=40 * 2**20
+                collective_id=0, has_side_effects=True, vmem_limit_bytes=60 * 2**20
             ),
             name="schwarz",
         )(source, permeability, storage, column_depth)

time: 70.8 us -> 67.1 us (0.948)
  local copies, waits for them, and re-layouts: 4.59 us -> 2.08 us
  Pallas kernels: 65.3 us -> 64.2 us
    unnamed x10 -> x4, local copies, waits for them, and re-layouts: 4.59 us -> 2.08 us
    pallas_call x1, Pallas kernels: 65.3 us -> 64.2 us  [per_device(): pl.pallas_call(functools.partial(kernel, sizes), out_shape=(jax.ShapeDtyp...]
where the time goes in v2:
time: 67.1 us; the launch traced here: 67 us
  Pallas kernels  64.2 us (96%)
  local copies, waits for them, and re-layouts  2.08 us (3%)
    pallas_call x1, Pallas kernels, per_device(): pl.pallas_call(functools.partial(kernel, sizes), out_shape=(jax.ShapeDtyp...  64.2 us
    unnamed x4, local copies, waits for them, and re-layouts  2.08 us

profile of v2, /device:TPU:1, one launch (start us, length us, event | category | flops | bytes accessed | tf_op | source)
XLA Modules:
  0.0 67.0 jit_solution(8183586893067961440)
XLA Ops:
  0.6 64.2 %schwarz.1 = (f32[8,32,128]{2,1,0:T(8,128)}, f32[3]{0:T(128)}) custom-call(f32[8,32,128]{2,1,0:T(8,128)} %src_hbm.1, f32[8,32,128]{2,1,0:T(8,128)} %perm_hbm.1, f32[8,32,128]{2,1,0:T(8,128)} %stor_hbm.1, s32[32,128]{1,0:T(8,128)} %depth_hbm.1), custom_call_target="tpu_custom_call" | custom-call | tf_op jit(solution)/shard_map/schwarz/pallas_call | solution.py:567
  64.9 0.0 copy-start
  64.9 1.6 %copy.8 = f32[8,32,128]{2,1,0:T(8,128)} copy(f32[8,32,128]{2,1,0:T(8,128)} %get-tuple-element.4) | data formatting | bytes 262144
  66.5 0.0 copy-done
  66.5 0.5 copy.9
Async XLA Ops:
  64.9 1.6 %copy-start = (f32[3]{0:T(128)S(1)}, f32[3]{0:T(128)}, u32[]{:S(2)}) copy-start(f32[3]{0:T(128)} %get-tuple-element.5) | copy-start | bytes 40

commit v3 on v2

v3 whole, which is shorter than its diff:
```python
import functools

import jax
import jax.numpy as jnp
from jax import lax
from jax.experimental import pallas as pl
from jax.experimental.pallas import tpu as pltpu
from jax.sharding import PartitionSpec as P

MESH = pl.DeviceIdType.MESH
ITERS = 3
RELAX = 0.9

PLANES, ROWS, LANES, PAD, STEP = 14, 40, 128, 8, 9
FLAT = PLANES * ROWS + 2 * PAD
SIDE = ROWS + 2 * PAD
DIRS = tuple(
    (sz, sx, sy)
    for sz in (-1, 0, 1)
    for sx in (-1, 0, 1)
    for sy in (-1, 0, 1)
    if (sz, sx, sy) != (0, 0, 0)
)
DIRS = tuple(sorted(DIRS, key=lambda s: -(abs(s[0]) + abs(s[1]) + abs(s[2]))))


def plane(z, count=1):
    return pl.ds(PAD + ROWS * z, ROWS * count)


MIDDLE = pl.ds(PAD, ROWS)


def iota(axis, shape=(ROWS, LANES)):
    return lax.broadcasted_iota(jnp.int32, shape, axis)


def roll(x, shift):
    return pltpu.roll(x, shift % LANES, axis=x.ndim - 1)


def both(*flags):
    return functools.reduce(jnp.logical_and, flags)


def either(*flags):
    return functools.reduce(jnp.logical_or, flags)


def between(x, low, high):
    return both(x >= low, x <= high)


def lanes_between(lane, low, high):
    if low < 0:
        return either(lane >= low + LANES, lane <= high)
    return between(lane, low, high)


def classes(shape, offset):
    u = lax.rem(iota(1, shape) + offset, LANES)
    z = (u * 57) >> 9
    return z, u - STEP * z


def row_tile(sx):
    return {0: pl.ds(0, ROWS), 1: pl.ds(ROWS - 8, 8), -1: pl.ds(0, 8)}[sx]


def add_tiles(acc, first, last):
    return jnp.concatenate([acc[:8] + first, acc[8 : ROWS - 8], acc[ROWS - 8 :] + last], axis=0)


def part_of(v):
    return (v + 1) // 2


def kernel(
    sizes, src_hbm, perm_hbm, stor_hbm, depth_hbm, out_hbm, hist_ref,
    in_src, in_perm, in_stor, in_depth, out_buf,
    own_rows, own_side, rz_k, rz_s, rz_q, rx0, rzx0, ry0, rxy0,
    send, rz, rx, rzx, ry, rxy,
    k_main, k_a, k_b, s_main, q_main,
    w_main, w_a, w_b, alpha, alpha_a, alpha_b, scale,
    r0_main, r0_a, r0_b, r_main, r_a, r_b, u_main, u_a, u_b, v_main, v_a, v_b, p_main, p_a, p_b,
    shifter, part, part_in,
    load_sem, out_sem, send0, recv0, sends, recvs, ar_send, ar_recv,
):
    n_gx, n_gy, n_gz = sizes
    gx, gy, gz = lax.axis_index("gx"), lax.axis_index("gy"), lax.axis_index("gz")

    def device(s):
        return (
            lax.rem(gx + s[1] + n_gx, n_gx),
            lax.rem(gy + s[2] + n_gy, n_gy),
            lax.rem(gz + s[0] + n_gz, n_gz),
        )

    barrier = pltpu.get_barrier_semaphore()
    for s in DIRS:
        pl.semaphore_signal(barrier, inc=1, device_id=device(s), device_id_type=MESH)

    loads = [
        pltpu.make_async_copy(a, b, load_sem.at[i])
        for i, (a, b) in enumerate(
            ((depth_hbm, in_depth), (perm_hbm, in_perm), (stor_hbm, in_stor), (src_hbm, in_src))
        )
    ]
    for copy in loads:
        copy.start()

    zero_plane = jnp.zeros((ROWS, LANES), jnp.float32)
    own_rows[...] = jnp.zeros(own_rows.shape, jnp.float32)
    own_side[...] = jnp.zeros(own_side.shape, jnp.float32)
    for ref in (k_main, s_main, q_main):
        ref[...] = jnp.zeros((FLAT, LANES), jnp.float32)
    for ref in (r0_main, r_main, u_main, v_main, p_main):
        ref[0 : PAD + ROWS] = jnp.zeros((PAD + ROWS, LANES), jnp.float32)
        ref[FLAT - PAD - ROWS :] = jnp.zeros((PAD + ROWS, LANES), jnp.float32)
    for ref in (k_a, k_b, r0_a, r0_b, r_a, r_b, u_a, u_b, v_a, v_b, p_a, p_b):
        ref[...] = jnp.zeros((SIDE, LANES), jnp.float32)

    at_in, at_out = iota(0, (2 * LANES, 2 * LANES)), iota(1, (2 * LANES, 2 * LANES))
    from_lane = lax.rem(at_out + jnp.where(at_out < LANES, LANES - 1, 1), LANES)
    shifter[...] = jnp.where(lax.rem(at_in, LANES) == from_lane, 1.0, 0.0).astype(jnp.bfloat16)

    lane, row = iota(1), iota(0)
    x = row - 4
    z_fa, y_fa = classes((ROWS, LANES), 0)
    z_fb, y_fb = classes((ROWS, LANES), 5)
    z_pa, y_pa = classes((ROWS, LANES), 1)
    z_pb, y_pb = classes((ROWS, LANES), 4)
    y_fa, y_fb, y_pa, y_pb = y_fa - 2, y_fb - 7, y_pa - 3, y_pb - 6

    def gather(accs, z, value):
        at = iota(1, value.shape)
        moved = roll(value, STEP * z + 2)
        return (
            jnp.where(lanes_between(at, STEP * z + 2, STEP * z + 8), moved, accs[0]),
            jnp.where(lanes_between(at, STEP * z - 5, STEP * z + 1), moved, accs[1]),
        )

    for copy in loads:
        copy.wait()

    depth = in_depth[...]
    zero_block = jnp.zeros((32, LANES), jnp.float32)
    edges = [(zero_block, zero_block)] * 3
    for z in range(8):
        in_perm[z] = jnp.where((gz * 8 + z) < depth, in_perm[z], 0.0)
        for f, ref in enumerate((in_perm, in_stor, in_src)):
            edges[f] = gather(edges[f], z + 3, ref[z])
        for v, low in ((0, 0), (1, 29)):
            own_rows[v, z, 0:3] = in_perm[z, low : low + 3]
            for i, ref in ((3, in_stor), (5, in_src)):
                own_rows[v, z, i : i + 2] = ref[z, low + v : low + v + 2]
    _, c = classes((32, LANES), 4)
    own_side[0, 4:36] = jnp.where(
        c >= 6, edges[0][0], jnp.where(c >= 3, roll(edges[1][0], -3), roll(edges[2][0], -6))
    )
    _, c = classes((32, LANES), 1)
    own_side[1, 4:36] = jnp.where(
        c < 3, edges[0][1], jnp.where(c < 6, roll(edges[1][1], 3), roll(edges[2][1], 6))
    )

    pl.semaphore_wait(barrier, len(DIRS))

    started = []
    exchange0 = []

    def post0(src, dst, s):
        i = len(exchange0)
        copy = pltpu.make_async_remote_copy(
            src_ref=src, dst_ref=dst, send_sem=send0.at[i], recv_sem=recv0.at[i],
            device_id=device(s), device_id_type=MESH,
        )
        copy.start()
        exchange0.append(copy)
        started.append(copy)

    for s in DIRS:
        sz, sx, sy = s
        u, v, d = part_of(sz), part_of(sx), part_of(sy)
        if sy == 0:
            if sz == 0:
                post0(own_rows.at[v], rx0.at[v], s)
            elif sx == 0:
                post0(in_perm.at[pl.ds(5 if sz > 0 else 0, 3)], rz_k.at[u], s)
                post0(in_stor.at[pl.ds(6 if sz > 0 else 0, 2)], rz_s.at[u], s)
                post0(in_src.at[pl.ds(6 if sz > 0 else 0, 2)], rz_q.at[u], s)
            else:
                post0(own_rows.at[v, pl.ds(5 if sz > 0 else 0, 3)], rzx0.at[u, v], s)
        elif sx == 0:
            post0(own_side.at[d], ry0.at[sz + 1, d], s)
        else:
            post0(own_side.at[d, row_tile(sx)], rxy0.at[sz + 1, v, d], s)
    for copy in exchange0:
        copy.wait_recv()

    def inside(flag):
        return flag.astype(jnp.float32)

    below, above = inside(gz > 0), inside(gz < n_gz - 1)
    before, after = inside(gx > 0), inside(gx < n_gx - 1)
    in_z = {z: below if z < 3 else above for z in (0, 1, 2, 11, 12, 13)}
    for z in range(PLANES):
        base = PAD + ROWS * z
        if 3 <= z <= 10:
            middle = in_perm[z - 3]
            low, high = rx0[1, z - 3], rx0[0, z - 3]
            gain = 1.0
            s_main[base + 4 : base + 36] = in_stor[z - 3]
            q_main[base + 4 : base + 36] = in_src[z - 3]
        else:
            u, i = (1, z) if z < 3 else (0, z - 11)
            middle = rz_k[u, i] * in_z[z]
            low, high = rzx0[u, 1, i], rzx0[u, 0, i]
            gain = in_z[z]
            if 1 <= z <= 12:
                i = z - 1 if z < 3 else z - 11
                s_main[base + 4 : base + 36] = rz_s[u, i]
                q_main[base + 4 : base + 36] = rz_q[u, i]
        k_main[base + 4 : base + 36] = middle
        k_main[base + 1 : base + 4] = low[0:3] * (before * gain)
        k_main[base + 36 : base + 39] = high[0:3] * (after * gain)
        s_main[base + 2 : base + 4] = low[3:5]
        s_main[base + 36 : base + 38] = high[3:5]
        q_main[base + 2 : base + 4] = low[5:7]
        q_main[base + 36 : base + 38] = high[5:7]

    def z_sum(here, lower, upper, offset, shift=0):
        z, _ = classes(here.shape, offset)
        moved = jnp.where(
            z <= 4, roll(lower, -8 * STEP - shift),
            jnp.where(both(z >= 9, z <= 13), roll(upper, 8 * STEP + shift), 0.0),
        )
        return here + moved

    def beside(y_ref, xy_ref, d):
        offset = 1 if d else 4
        return add_tiles(
            z_sum(y_ref(1, d), y_ref(2, d), y_ref(0, d), offset),
            z_sum(xy_ref(1, 1, d), xy_ref(2, 1, d), xy_ref(0, 1, d), offset),
            z_sum(xy_ref(1, 0, d), xy_ref(2, 0, d), xy_ref(0, 0, d), offset),
        )

    from_left, from_right = (
        beside(lambda i, d: ry0[i, d], lambda i, v, d: rxy0[i, v, d], d) for d in (1, 0)
    )

    def grid_z(z):
        return both(either(z >= 3, gz > 0), either(z <= 10, gz < n_gz - 1))

    row_in = both(either(x >= 0, gx > 0), either(x < 32, gx < n_gx - 1))
    gain_a = jnp.where(both(row_in, grid_z(z_pa), gy > 0), 1.0, 0.0)
    gain_b = jnp.where(both(row_in, grid_z(z_pb), gy < n_gy - 1), 1.0, 0.0)
    k_edges, s_edges, q_edges = ((zero_plane, zero_plane) for _ in range(3))
    for z in range(PLANES):
        k_edges = gather(k_edges, z, k_main[plane(z)])
        if 1 <= z <= 12:
            s_edges = gather(s_edges, z, s_main[plane(z)])
            q_edges = gather(q_edges, z, q_main[plane(z)])
    k_left, k_right = from_left * gain_a, from_right * gain_b
    k_fa = jnp.where(both(y_pa >= -2, y_pa <= -1), k_left, k_edges[0])
    k_fb = jnp.where(both(y_pb >= 0, y_pb <= 1), k_right, k_edges[1])
    k_pa = jnp.where(y_pa == -3, k_left, k_fa)
    k_pb = jnp.where(y_pb == 2, k_right, k_fb)
    k_a[MIDDLE] = k_fa
    k_b[MIDDLE] = k_fb
    s_a = jnp.where(both(y_pa >= -2, y_pa <= -1), roll(from_left, -3), s_edges[0])
    q_a = jnp.where(both(y_pa >= -2, y_pa <= -1), roll(from_left, -6), q_edges[0])
    s_b = jnp.where(both(y_pb >= 0, y_pb <= 1), roll(from_right, 3), s_edges[1])
    q_b = jnp.where(both(y_pb >= 0, y_pb <= 1), roll(from_right, 6), q_edges[1])

    def weights(centre, others, storage, source, keep):
        idle = jnp.where(centre > 0.0, 0.0, 1.0)
        diagonal = storage + idle
        couplings = []
        for other in others:
            other_idle = jnp.where(other > 0.0, 0.0, 1.0)
            c = (2.0 * centre) * other / ((centre + idle) + (other + other_idle))
            couplings.append(c)
            diagonal = diagonal + c
        gain = jnp.where(keep, RELAX / diagonal, 0.0)
        live = jnp.where(keep, 1.0 - idle, 0.0)
        return [c * gain for c in couplings], live * gain * source, live * RELAX, diagonal

    def around(ref, z, count=1):
        base, rows = PAD + ROWS * z, ROWS * count
        return (
            ref[pl.ds(base - ROWS, rows)],
            ref[pl.ds(base + ROWS, rows)],
            ref[pl.ds(base - 1, rows)],
            ref[pl.ds(base + 1, rows)],
        )

    def side_around(ref, centre):
        return (
            roll(centre, STEP), roll(centre, -STEP), ref[pl.ds(PAD - 1, ROWS)], ref[pl.ds(PAD + 1, ROWS)],
        )

    rows_kept, rows_own = between(row, 2, 37), between(row, 4, 35)
    inner = both(lane > 0, lane < LANES - 1)
    total = zero_plane
    r_edges = (zero_plane, zero_plane)
    for z in range(1, 13):
        centre = k_main[plane(z)]
        ws, r, al, diagonal = weights(
            centre, around(k_main, z) + (roll(centre, 1), roll(centre, -1)),
            s_main[plane(z)], q_main[plane(z)], rows_kept,
        )
        for i in range(6):
            w_main[i, plane(z)] = ws[i]
        alpha[plane(z)] = al
        r0_main[plane(z)] = r
        r_edges = gather(r_edges, z, r)
        if 3 <= z <= 10:
            sc = jnp.where(both(rows_own, inner), diagonal * (1.0 / RELAX), 0.0)
            scale[z - 3] = sc
            total = total + (r * sc) * (r * sc)
    scale_side = []
    for ref, k_f, left, right, st, q, z, y, low, high, w_ref, al_ref, r_ref, edge, own in (
        (k_a, k_fa, k_pa, k_fa, s_a, q_a, z_fa, y_fa, -2, 5, w_a, alpha_a, r0_a, r_edges[0], 0),
        (k_b, k_fb, k_fb, k_pb, s_b, q_b, z_fb, y_fb, -6, 1, w_b, alpha_b, r0_b, r_edges[1], -1),
    ):
        keep = both(rows_kept, between(z, 1, 12), between(y, low, high))
        ws, r, al, diagonal = weights(
            k_f, side_around(ref, k_f) + (roll(left, 1), roll(right, -1)), st, q, keep
        )
        for i in range(6):
            w_ref[i] = ws[i]
        if low == -2:
            w_ref[6] = jnp.where(y == -2, 0.0, ws[4])
        else:
            w_ref[6] = jnp.where(y == 1, 0.0, ws[5])
        al_ref[...] = al
        r_ref[MIDDLE] = jnp.where(y <= 0 if low == -2 else y >= -1, r, edge)
        sc = jnp.where(
            both(rows_own, between(z, 3, 10), y == own), diagonal * (1.0 / RELAX), 0.0
        )
        scale_side.append(sc)
        total = total + (r * sc) * (r * sc)

    def half(flag):
        return jnp.where(flag, 0.5, 1.0)

    def axis_gain(position, extent, owner, owners):
        inner_low = both(position >= 0, position < 2, owner > 0)
        inner_high = both(position >= extent - 2, position < extent, owner < owners - 1)
        outer = either(
            both(position >= -2, position < 0), both(position >= extent, position < extent + 2)
        )
        return half(either(outer, inner_low, inner_high))

    x_gain = axis_gain(x, 32, gx, n_gx)
    main_gain = x_gain * axis_gain(lane, 128, gy, n_gy)
    side_gain = (
        x_gain * axis_gain(z_pa - 3, 8, gz, n_gz) * axis_gain(y_pa, 128, gy, n_gy),
        x_gain * axis_gain(z_pb - 3, 8, gz, n_gz) * axis_gain(y_pb + 128, 128, gy, n_gy),
    )

    def z_gain(z):
        if z in (0, 13):
            return 1.0
        if z in (1, 2, 11, 12):
            return 0.5
        if z in (3, 4):
            return jnp.where(gz > 0, 0.5, 1.0)
        if z in (9, 10):
            return jnp.where(gz < n_gz - 1, 0.5, 1.0)
        return 1.0

    def side_sweep(ref, rhs, w_ref, last):
        value = ref[MIDDLE]
        others = side_around(ref, value) + (roll(value, 1), roll(value, -1))
        value = (1.0 - RELAX) * value + rhs[MIDDLE]
        for i, other in enumerate(others):
            value = value + w_ref[6 if i == last else i] * other
        return value

    def main_sweep(ref, rhs, z):
        value = ref[plane(z, 2)]
        hi = value.astype(jnp.bfloat16)
        lo = (value - hi.astype(jnp.float32)).astype(jnp.bfloat16)
        beside_y = jnp.dot(
            jnp.concatenate([hi, lo], axis=1), shifter[...], preferred_element_type=jnp.float32
        )
        others = around(ref, z, 2) + (beside_y[:, :LANES], beside_y[:, LANES:])
        value = (1.0 - RELAX) * value + rhs[plane(z, 2)]
        for i, other in enumerate(others):
            value = value + w_main[i, plane(z, 2)] * other
        return value

    partials = [total]
    for k in range(ITERS):
        rhs, rhs_a, rhs_b = (r0_main, r0_a, r0_b) if k == 0 else (r_main, r_a, r_b)
        copies = []

        def post(source, target, s):
            i = DIRS.index(s)
            copy = pltpu.make_async_remote_copy(
                src_ref=source, dst_ref=target, send_sem=sends.at[k, i], recv_sem=recvs.at[k, i],
                device_id=device(s), device_id_type=MESH,
            )
            copy.start()
            copies.append(copy)
            started.append(copy)

        for before_ref, after_ref in (((rhs_a, rhs_b), (u_a, u_b)), ((u_a, u_b), (v_a, v_b))):
            after_ref[0][MIDDLE] = side_sweep(before_ref[0], rhs_a, w_a, 4)
            after_ref[1][MIDDLE] = side_sweep(before_ref[1], rhs_b, w_b, 5)
        side_a = side_sweep(v_a, rhs_a, w_a, 4)
        side_b = side_sweep(v_b, rhs_b, w_b, 5)
        far_b = roll(side_b, 64)
        send[k, 0] = jnp.where(lane < 60, side_a, far_b)
        send[k, 13] = jnp.where(lane < 60, far_b, side_a)
        send[k, 14] = side_a
        send[k, 15] = side_b
        for s in DIRS:
            sz, sx, sy = s
            v, d = part_of(sx), part_of(sy)
            if sy != 0:
                source = send.at[k, 15 if sy > 0 else 14, row_tile(sx)]
                post(source, ry.at[k, sz + 1, d] if sx == 0 else rxy.at[k, sz + 1, v, d], s)

        for z in range(1, 13, 2):
            u_main[plane(z, 2)] = main_sweep(rhs, rhs, z)
        for z in range(1, 13, 2):
            v_main[plane(z, 2)] = main_sweep(u_main, rhs, z)
        for z in (1, 3, 5, 11, 9, 7):
            value = main_sweep(v_main, rhs, z)
            send[k, z] = value[:ROWS]
            send[k, z + 1] = value[ROWS:]
            if z in (5, 7):
                sz = -1 if z == 5 else 1
                planes = pl.ds(0 if z == 5 else 8, 6)
                for sx in (-1, 1):
                    post(
                        send.at[k, planes, row_tile(sx)],
                        rzx.at[k, part_of(sz), part_of(sx)], (sz, sx, 0),
                    )
                post(send.at[k, planes], rz.at[k, part_of(sz)], (sz, 0, 0))
        for sx in (-1, 1):
            post(send.at[k, pl.ds(1, 15), row_tile(sx)], rx.at[k, part_of(sx)], (0, sx, 0))
        for copy in copies:
            copy.wait_recv()

        new_p = []
        for own, d, offset, shift, y, low, high, outer_low, outer_high, ref in (
            (14, 1, 1, 0, y_pa, -2, 3, -3, 1, p_a),
            (15, 0, 4, 64, y_pb, -4, 1, -2, 2, p_b),
        ):
            here = add_tiles(
                z_sum(send[k, own], rz[k, 1, 5], rz[k, 0, 0], offset, shift),
                z_sum(rx[k, 1, own - 1], rzx[k, 1, 1, 5], rzx[k, 0, 1, 0], offset, shift),
                z_sum(rx[k, 0, own - 1], rzx[k, 1, 0, 5], rzx[k, 0, 0, 0], offset, shift),
            )
            other = beside(lambda i, d: ry[k, i, d], lambda i, v, d: rxy[k, i, v, d], d)
            value = jnp.where(between(y, low, high), here, 0.0) + jnp.where(
                between(y, outer_low, outer_high), other, 0.0
            )
            value = value * side_gain[1 - d]
            if k > 0:
                value = ref[MIDDLE] + value
            ref[MIDDLE] = value
            new_p.append(value)
        edges = jnp.where(between(y_pa, 0, 3), new_p[0], new_p[1])
        edge_lane = either(lane < 4, lane >= LANES - 4)
        for z in range(PLANES):
            solved = 1 <= z <= 12
            value = send[k, z] if solved else zero_plane
            first = rx[k, 1, z - 1] if solved else jnp.zeros((8, LANES), jnp.float32)
            last = rx[k, 0, z - 1] if solved else jnp.zeros((8, LANES), jnp.float32)
            if z <= 4:
                value = value + rz[k, 1, z]
                first = first + rzx[k, 1, 1, z]
                last = last + rzx[k, 1, 0, z]
            if z >= 9:
                value = value + rz[k, 0, z - 8]
                first = first + rzx[k, 0, 1, z - 8]
                last = last + rzx[k, 0, 0, z - 8]
            value = add_tiles(value, first, last) * (main_gain * z_gain(z))
            if k > 0:
                value = p_main[plane(z)] + value
            p_main[plane(z)] = jnp.where(edge_lane, roll(edges, -(STEP * z + 2)), value)

        total = zero_plane
        r_edges = (zero_plane, zero_plane)
        last_one = k == ITERS - 1
        for z in range(3, 11) if last_one else range(1, 13):
            centre = p_main[plane(z)]
            value = r0_main[plane(z)] - alpha[plane(z)] * centre
            for i, other in enumerate(
                around(p_main, z) + (roll(centre, 1), roll(centre, -1))
            ):
                value = value + w_main[i, plane(z)] * other
            if not last_one:
                r_main[plane(z)] = value
                r_edges = gather(r_edges, z, value)
            if 3 <= z <= 10:
                value = value * scale[z - 3]
                total = total + value * value
        for i, (ref, r0, al, w_ref, r_ref, p) in enumerate(
            ((p_a, r0_a, alpha_a, w_a, r_a, new_p[0]), (p_b, r0_b, alpha_b, w_b, r_b, new_p[1]))
        ):
            value = r0[MIDDLE] - al[...] * p
            for n, other in enumerate(side_around(ref, p) + (roll(p, 1), roll(p, -1))):
                value = value + w_ref[n] * other
            if not last_one:
                r_ref[MIDDLE] = jnp.where(y_fa <= 0 if i == 0 else y_fb >= -1, value, r_edges[i])
            value = value * scale_side[i]
            total = total + value * value
        partials.append(total)

    for z in range(8):
        out_buf[z] = p_main[pl.ds(PAD + ROWS * (z + 3) + 4, 32)]
    out_copy = pltpu.make_async_copy(out_buf, out_hbm, out_sem)
    out_copy.start()

    at = iota(1, (1, LANES)) // 32
    mine = jnp.zeros((1, LANES), jnp.float32)
    for i, value in enumerate(partials):
        value = jnp.sum(value, axis=0, keepdims=True)
        value = value + roll(value, 64)
        mine = jnp.where(at == i, value + roll(value, 32), mine)
    pair = gy + 1 - 2 * lax.rem(gy, 2)

    def ring(i, n):
        return min(i, n - i)

    rounds = (
        sorted(
            ((i, h) for i in range(n_gx) for h in range(2) if (i, h) != (0, 0)),
            key=lambda t: -ring(t[0], n_gx) - 0.3 * t[1],
        ),
        sorted(
            ((i, h) for i in range(n_gy // 2) for h in range(n_gz) if (i, h) != (0, 0)),
            key=lambda t: -ring(t[0], n_gy // 2) - ring(t[1], n_gz),
        ),
    )
    rounds = (
        [(lax.rem(gx + i, n_gx), gy if h == 0 else pair, gz) for i, h in rounds[0]],
        [(gx, lax.rem(gy + 2 * i, n_gy), lax.rem(gz + h, n_gz)) for i, h in rounds[1]],
    )
    slots = (gx * 2 + lax.rem(gy, 2), (gy // 2) * n_gz + gz)
    for n, targets in enumerate(rounds):
        here = part_in.at[n, slots[n], pl.ds(0, 1)]
        part[n, 0:1] = mine
        copies = []
        for i, target in enumerate(targets):
            copy = pltpu.make_async_remote_copy(
                src_ref=part.at[n, pl.ds(0, 1)], dst_ref=here,
                send_sem=ar_send.at[n, i], recv_sem=ar_recv.at[n, i],
                device_id=target, device_id_type=MESH,
            )
            copy.start()
            copies.append(copy)
            started.append(copy)
        here[...] = mine
        for copy in copies:
            copy.wait_recv()
        terms = [part_in[n, i, 0:1] for i in range(len(targets) + 1)]
        while len(terms) > 1:
            terms = [sum(terms[i + 1 : i + 2], terms[i]) for i in range(0, len(terms), 2)]
        mine = terms[0]
    squares = [
        jnp.sum(jnp.where(at == i, mine, 0.0), axis=1, keepdims=True) for i in range(ITERS + 1)
    ]
    for i in range(ITERS):
        hist_ref[i] = jnp.sum(jnp.sqrt(squares[i + 1] / squares[0]))
    out_copy.wait()
    for copy in started:
        copy.wait_send()


def solution(mesh):
    sizes = (mesh.shape["gx"], mesh.shape["gy"], mesh.shape["gz"])
    f32 = jnp.float32

    def vmem(*shape):
        return pltpu.VMEM(shape, f32)

    n_dirs = len(DIRS)
    n_first = n_dirs + 4
    scratch = [
        vmem(8, 32, LANES), vmem(8, 32, LANES), vmem(8, 32, LANES),
        pltpu.VMEM((32, LANES), jnp.int32), vmem(8, 32, LANES),
        vmem(2, 8, 8, LANES), vmem(2, ROWS, LANES),
        vmem(2, 3, 32, LANES), vmem(2, 2, 32, LANES), vmem(2, 2, 32, LANES),
        vmem(2, 8, 8, LANES), vmem(2, 2, 3, 8, LANES),
        vmem(3, 2, ROWS, LANES), vmem(3, 2, 2, 8, LANES),
        vmem(ITERS, 16, ROWS, LANES),
        vmem(ITERS, 2, 6, ROWS, LANES), vmem(ITERS, 2, 15, 8, LANES),
        vmem(ITERS, 2, 2, 6, 8, LANES),
        vmem(ITERS, 3, 2, ROWS, LANES), vmem(ITERS, 3, 2, 2, 8, LANES),
        vmem(FLAT, LANES), vmem(SIDE, LANES), vmem(SIDE, LANES), vmem(FLAT, LANES), vmem(FLAT, LANES),
        vmem(6, FLAT, LANES), vmem(7, ROWS, LANES), vmem(7, ROWS, LANES),
        vmem(FLAT, LANES), vmem(ROWS, LANES), vmem(ROWS, LANES), vmem(8, ROWS, LANES),
    ]
    for _ in range(5):
        scratch += [vmem(FLAT, LANES), vmem(SIDE, LANES), vmem(SIDE, LANES)]
    scratch += [
        pltpu.VMEM((2 * LANES, 2 * LANES), jnp.bfloat16),
        vmem(2, 8, LANES), vmem(2, 16, 8, LANES),
        pltpu.SemaphoreType.DMA((4,)), pltpu.SemaphoreType.DMA,
        pltpu.SemaphoreType.DMA((n_first,)), pltpu.SemaphoreType.DMA((n_first,)),
        pltpu.SemaphoreType.DMA((ITERS, n_dirs)), pltpu.SemaphoreType.DMA((ITERS, n_dirs)),
        pltpu.SemaphoreType.DMA((2, 15)), pltpu.SemaphoreType.DMA((2, 15)),
    ]

    def per_device(source, permeability, storage, column_depth):
        return pl.pallas_call(
            functools.partial(kernel, sizes),
            out_shape=(
                jax.ShapeDtypeStruct(source.shape, f32),
                jax.ShapeDtypeStruct((ITERS,), f32),
            ),
            in_specs=[pl.BlockSpec(memory_space=pl.ANY)] * 4,
            out_specs=(
                pl.BlockSpec(memory_space=pl.ANY),
                pl.BlockSpec(memory_space=pltpu.SMEM),
            ),
            scratch_shapes=scratch,
            compiler_params=pltpu.CompilerParams(
                collective_id=0, has_side_effects=True, vmem_limit_bytes=60 * 2**20
            ),
            name="schwarz",
        )(source, permeability, storage, column_depth)

    placed = (P("gz", "gx", "gy"), P("gz", "gx", "gy"), P("gz", "gx", "gy"), P("gx", "gy"))
    return jax.shard_map(
        per_device,
        mesh=mesh,
        in_specs=placed,
        out_specs=(P("gz", "gx", "gy"), P()),
        check_vma=False,
    )
```

time: 67.1 us -> 56.8 us (0.85)
  Pallas kernels: 64.2 us -> 53.9 us
    pallas_call x1, Pallas kernels: 64.2 us -> 53.9 us  [per_device(): pl.pallas_call(functools.partial(kernel, sizes), out_shape=(jax.ShapeDtyp...]
where the time goes in v3:
time: 56.8 us; the launch traced here: 56.6 us
  Pallas kernels  53.9 us (95%)
  local copies, waits for them, and re-layouts  2.08 us (4%)
  between operations  0.65 us (1%)
    pallas_call x1, Pallas kernels, per_device(): pl.pallas_call(functools.partial(kernel, sizes), out_shape=(jax.ShapeDtyp...  53.9 us
    unnamed x4, local copies, waits for them, and re-layouts  2.08 us

profile of v3, /device:TPU:1, one launch (start us, length us, event | category | flops | bytes accessed | tf_op | source)
XLA Modules:
  0.0 56.6 jit_solution(9681303762359619469)
XLA Ops:
  0.6 53.9 %schwarz.1 = (f32[8,32,128]{2,1,0:T(8,128)}, f32[3]{0:T(128)}) custom-call(f32[8,32,128]{2,1,0:T(8,128)} %src_hbm.1, f32[8,32,128]{2,1,0:T(8,128)} %perm_hbm.1, f32[8,32,128]{2,1,0:T(8,128)} %stor_hbm.1, s32[32,128]{1,0:T(8,128)} %depth_hbm.1), custom_call_target="tpu_custom_call" | custom-call | tf_op jit(solution)/shard_map/schwarz/pallas_call | solution.py:612
  54.5 0.0 copy-start
  54.6 1.6 %copy.8 = f32[8,32,128]{2,1,0:T(8,128)} copy(f32[8,32,128]{2,1,0:T(8,128)} %get-tuple-element.4) | data formatting | bytes 262144
  56.1 0.0 copy-done
  56.1 0.5 copy.9
Async XLA Ops:
  54.5 1.6 %copy-start = (f32[3]{0:T(128)S(1)}, f32[3]{0:T(128)}, u32[]{:S(2)}) copy-start(f32[3]{0:T(128)} %get-tuple-element.5) | copy-start | bytes 40

commit v4 on v3

--- a/solution.py
+++ b/solution.py
@@ -71,20 +71,40 @@
     return jnp.concatenate([acc[:8] + first, acc[8 : ROWS - 8], acc[ROWS - 8 :] + last], axis=0)
 
 
+WIDTH = 43
+
+
+def fold(side, first):
+    t = [side[8 * i : 8 * i + 8] for i in range(5)]
+    at = lax.rem(iota(1, (8, LANES)) + (LANES - first), LANES)
+    one = jnp.where(
+        at < WIDTH, t[0], jnp.where(at < 2 * WIDTH, roll(t[1], WIDTH), roll(t[2], 2 * WIDTH))
+    )
+    two = jnp.where(at < WIDTH, t[3], roll(t[4], WIDTH))
+    return jnp.concatenate([one, two], axis=0)
+
+
+def unfold(both_tiles, shift):
+    return jnp.concatenate(
+        [roll(both_tiles[8 * (i // 3) : 8 * (i // 3) + 8], shift - WIDTH * (i % 3)) for i in range(5)],
+        axis=0,
+    )
+
+
 def part_of(v):
     return (v + 1) // 2
 
 
 def kernel(
-    sizes, src_hbm, perm_hbm, stor_hbm, depth_hbm, out_hbm, hist_ref,
-    in_src, in_perm, in_stor, in_depth, out_buf,
-    own_rows, own_side, rz_k, rz_s, rz_q, rx0, rzx0, ry0, rxy0,
-    send, rz, rx, rzx, ry, rxy,
+    sizes, src_hbm, perm_hbm, stor_hbm, depth_hbm, out_ref, hist_ref,
+    in_src, in_perm, in_stor, in_depth,
+    own_rows, own_side, own_fold, rz_k, rz_s, rz_q, rx0, rzx0, ry0, rzy0, rxy0,
+    send, zx_out, fold_out, rz, rx, rzx, ry, rzy, rxy,
     k_main, k_a, k_b, s_main, q_main,
     w_main, w_a, w_b, alpha, alpha_a, alpha_b, scale,
     r0_main, r0_a, r0_b, r_main, r_a, r_b, u_main, u_a, u_b, v_main, v_a, v_b, p_main, p_a, p_b,
     shifter, part, part_in,
-    load_sem, out_sem, send0, recv0, sends, recvs, ar_send, ar_recv,
+    load_sem, send0, recv0, sends, recvs, ar_send, ar_recv,
 ):
     n_gx, n_gy, n_gz = sizes
     gx, gy, gz = lax.axis_index("gx"), lax.axis_index("gy"), lax.axis_index("gz")
@@ -144,10 +164,32 @@
         copy.wait()
 
     depth = in_depth[...]
+    for z in range(8):
+        in_perm[z] = jnp.where((gz * 8 + z) < depth, in_perm[z], 0.0)
+
+    pl.semaphore_wait(barrier, len(DIRS))
+
+    started = []
+    exchange0 = []
+
+    def post0(src, dst, s):
+        i = len(exchange0)
+        copy = pltpu.make_async_remote_copy(
+            src_ref=src, dst_ref=dst, send_sem=send0.at[i], recv_sem=recv0.at[i],
+            device_id=device(s), device_id_type=MESH,
+        )
+        copy.start()
+        exchange0.append(copy)
+        started.append(copy)
+
+    for sz in (-1, 1):
+        u = part_of(sz)
+        post0(in_perm.at[pl.ds(5 * u, 3)], rz_k.at[u], (sz, 0, 0))
+        post0(in_stor.at[pl.ds(6 * u, 2)], rz_s.at[u], (sz, 0, 0))
+        post0(in_src.at[pl.ds(6 * u, 2)], rz_q.at[u], (sz, 0, 0))
     zero_block = jnp.zeros((32, LANES), jnp.float32)
     edges = [(zero_block, zero_block)] * 3
     for z in range(8):
-        in_perm[z] = jnp.where((gz * 8 + z) < depth, in_perm[z], 0.0)
         for f, ref in enumerate((in_perm, in_stor, in_src)):
             edges[f] = gather(edges[f], z + 3, ref[z])
         for v, low in ((0, 0), (1, 29)):
@@ -162,38 +204,23 @@
     own_side[1, 4:36] = jnp.where(
         c < 3, edges[0][1], jnp.where(c < 6, roll(edges[1][1], 3), roll(edges[2][1], 6))
     )
-
-    pl.semaphore_wait(barrier, len(DIRS))
-
-    started = []
-    exchange0 = []
-
-    def post0(src, dst, s):
-        i = len(exchange0)
-        copy = pltpu.make_async_remote_copy(
-            src_ref=src, dst_ref=dst, send_sem=send0.at[i], recv_sem=recv0.at[i],
-            device_id=device(s), device_id_type=MESH,
-        )
-        copy.start()
-        exchange0.append(copy)
-        started.append(copy)
-
+    for d in range(2):
+        for u in range(2):
+            own_fold[u, d] = fold(own_side[d], STEP * (8 if u else 3) - (1 if d else 4))
     for s in DIRS:
         sz, sx, sy = s
         u, v, d = part_of(sz), part_of(sx), part_of(sy)
         if sy == 0:
             if sz == 0:
                 post0(own_rows.at[v], rx0.at[v], s)
-            elif sx == 0:
-                post0(in_perm.at[pl.ds(5 if sz > 0 else 0, 3)], rz_k.at[u], s)
-                post0(in_stor.at[pl.ds(6 if sz > 0 else 0, 2)], rz_s.at[u], s)
-                post0(in_src.at[pl.ds(6 if sz > 0 else 0, 2)], rz_q.at[u], s)
-            else:
-                post0(own_rows.at[v, pl.ds(5 if sz > 0 else 0, 3)], rzx0.at[u, v], s)
-        elif sx == 0:
-            post0(own_side.at[d], ry0.at[sz + 1, d], s)
+            elif sx != 0:
+                post0(own_rows.at[v, pl.ds(5 * u, 3)], rzx0.at[u, v], s)
+        elif sx != 0:
+            post0(own_side.at[d, row_tile(sx)], rxy0.at[sz + 1, v, d], s)
+        elif sz != 0:
+            post0(own_fold.at[u, d], rzy0.at[u, d], s)
         else:
-            post0(own_side.at[d, row_tile(sx)], rxy0.at[sz + 1, v, d], s)
+            post0(own_side.at[d], ry0.at[d], s)
     for copy in exchange0:
         copy.wait_recv()
 
@@ -228,25 +255,23 @@
         q_main[base + 2 : base + 4] = low[5:7]
         q_main[base + 36 : base + 38] = high[5:7]
 
-    def z_sum(here, lower, upper, offset, shift=0):
+    def z_sum(here, lower, upper, offset, shift=0, move=roll, reach=5):
         z, _ = classes(here.shape, offset)
         moved = jnp.where(
-            z <= 4, roll(lower, -8 * STEP - shift),
-            jnp.where(both(z >= 9, z <= 13), roll(upper, 8 * STEP + shift), 0.0),
+            z < reach, move(lower, -8 * STEP - shift),
+            jnp.where(between(z, 14 - reach, 13), move(upper, 8 * STEP + shift), 0.0),
         )
         return here + moved
 
-    def beside(y_ref, xy_ref, d):
+    def beside(y, zy, xy, d, reach=5):
         offset = 1 if d else 4
         return add_tiles(
-            z_sum(y_ref(1, d), y_ref(2, d), y_ref(0, d), offset),
-            z_sum(xy_ref(1, 1, d), xy_ref(2, 1, d), xy_ref(0, 1, d), offset),
-            z_sum(xy_ref(1, 0, d), xy_ref(2, 0, d), xy_ref(0, 0, d), offset),
-        )
-
-    from_left, from_right = (
-        beside(lambda i, d: ry0[i, d], lambda i, v, d: rxy0[i, v, d], d) for d in (1, 0)
-    )
+            z_sum(y[d], zy[1, d], zy[0, d], offset, move=unfold, reach=reach),
+            z_sum(xy[1, 1, d], xy[2, 1, d], xy[0, 1, d], offset, reach=reach),
+            z_sum(xy[1, 0, d], xy[2, 0, d], xy[0, 0, d], offset, reach=reach),
+        )
+
+    from_left, from_right = (beside(ry0, rzy0, rxy0, d, 3) for d in (1, 0))
 
     def grid_z(z):
         return both(either(z >= 3, gz > 0), either(z <= 10, gz < n_gz - 1))
@@ -395,6 +420,7 @@
     for k in range(ITERS):
         rhs, rhs_a, rhs_b = (r0_main, r0_a, r0_b) if k == 0 else (r_main, r_a, r_b)
         copies = []
+        last_one = k == ITERS - 1
 
         def post(source, target, s):
             i = DIRS.index(s)
@@ -416,12 +442,19 @@
         send[k, 13] = jnp.where(lane < 60, far_b, side_a)
         send[k, 14] = side_a
         send[k, 15] = side_b
+        for d, value in ((0, side_a), (1, side_b)):
+            for u in range(2):
+                fold_out[k, u, d] = fold(value, STEP * (8 if u else 1) - d)
         for s in DIRS:
             sz, sx, sy = s
-            v, d = part_of(sx), part_of(sy)
+            u, v, d = part_of(sz), part_of(sx), part_of(sy)
             if sy != 0:
-                source = send.at[k, 15 if sy > 0 else 14, row_tile(sx)]
-                post(source, ry.at[k, sz + 1, d] if sx == 0 else rxy.at[k, sz + 1, v, d], s)
+                if sx != 0:
+                    post(send.at[k, 14 + d, row_tile(sx)], rxy.at[k, sz + 1, v, d], s)
+                elif sz != 0:
+                    post(fold_out.at[k, u, d], rzy.at[k, u, d], s)
+                else:
+                    post(send.at[k, 14 + d], ry.at[k, d], s)
 
         for z in range(1, 13, 2):
             u_main[plane(z, 2)] = main_sweep(rhs, rhs, z)
@@ -433,17 +466,28 @@
             send[k, z + 1] = value[ROWS:]
             if z in (5, 7):
                 sz = -1 if z == 5 else 1
-                planes = pl.ds(0 if z == 5 else 8, 6)
-                for sx in (-1, 1):
+                count = 4 if last_one else 6
+                skip = 6 - count if sz > 0 else 0
+                planes, places = pl.ds((8 if sz > 0 else 0) + skip, count), pl.ds(skip, count)
+                u = part_of(sz)
+                for v, low in ((0, 2), (1, 33)):
+                    for i in range(6):
+                        zx_out[k, u, v, 2 + 5 * i : 7 + 5 * i] = send[
+                            k, (8 + i) if u else i, low : low + 5
+                        ]
                     post(
-                        send.at[k, planes, row_tile(sx)],
-                        rzx.at[k, part_of(sz), part_of(sx)], (sz, sx, 0),
+                        zx_out.at[k, u, v], rzx.at[k, u, v, pl.ds(0, 32)], (sz, 2 * v - 1, 0)
                     )
-                post(send.at[k, planes], rz.at[k, part_of(sz)], (sz, 0, 0))
+                post(send.at[k, planes], rz.at[k, part_of(sz), places], (sz, 0, 0))
         for sx in (-1, 1):
             post(send.at[k, pl.ds(1, 15), row_tile(sx)], rx.at[k, part_of(sx)], (0, sx, 0))
         for copy in copies:
             copy.wait_recv()
+
+        def edge_rows(u, v, i):
+            at = iota(0, (8, LANES))
+            tile = rzx[k, u, v, 5 * i + v : 5 * i + v + 8]
+            return jnp.where(between(at, 2 - v, 6 - v), tile, 0.0)
 
         new_p = []
         for own, d, offset, shift, y, low, high, outer_low, outer_high, ref in (
@@ -452,10 +496,10 @@
         ):
             here = add_tiles(
                 z_sum(send[k, own], rz[k, 1, 5], rz[k, 0, 0], offset, shift),
-                z_sum(rx[k, 1, own - 1], rzx[k, 1, 1, 5], rzx[k, 0, 1, 0], offset, shift),
-                z_sum(rx[k, 0, own - 1], rzx[k, 1, 0, 5], rzx[k, 0, 0, 0], offset, shift),
+                z_sum(rx[k, 1, own - 1], edge_rows(1, 1, 5), edge_rows(0, 1, 0), offset, shift),
+                z_sum(rx[k, 0, own - 1], edge_rows(1, 0, 5), edge_rows(0, 0, 0), offset, shift),
             )
-            other = beside(lambda i, d: ry[k, i, d], lambda i, v, d: rxy[k, i, v, d], d)
+            other = beside(ry.at[k], rzy.at[k], rxy.at[k], d)
             value = jnp.where(between(y, low, high), here, 0.0) + jnp.where(
                 between(y, outer_low, outer_high), other, 0.0
             )
@@ -466,19 +510,19 @@
             new_p.append(value)
         edges = jnp.where(between(y_pa, 0, 3), new_p[0], new_p[1])
         edge_lane = either(lane < 4, lane >= LANES - 4)
-        for z in range(PLANES):
+        for z in range(2, 12) if last_one else range(PLANES):
             solved = 1 <= z <= 12
             value = send[k, z] if solved else zero_plane
             first = rx[k, 1, z - 1] if solved else jnp.zeros((8, LANES), jnp.float32)
             last = rx[k, 0, z - 1] if solved else jnp.zeros((8, LANES), jnp.float32)
             if z <= 4:
                 value = value + rz[k, 1, z]
-                first = first + rzx[k, 1, 1, z]
-                last = last + rzx[k, 1, 0, z]
+                first = first + edge_rows(1, 1, z)
+                last = last + edge_rows(1, 0, z)
             if z >= 9:
                 value = value + rz[k, 0, z - 8]
-                first = first + rzx[k, 0, 1, z - 8]
-                last = last + rzx[k, 0, 0, z - 8]
+                first = first + edge_rows(0, 1, z - 8)
+                last = last + edge_rows(0, 0, z - 8)
             value = add_tiles(value, first, last) * (main_gain * z_gain(z))
             if k > 0:
                 value = p_main[plane(z)] + value
@@ -486,7 +530,6 @@
 
         total = zero_plane
         r_edges = (zero_plane, zero_plane)
-        last_one = k == ITERS - 1
         for z in range(3, 11) if last_one else range(1, 13):
             centre = p_main[plane(z)]
             value = r0_main[plane(z)] - alpha[plane(z)] * centre
@@ -513,9 +556,7 @@
         partials.append(total)
 
     for z in range(8):
-        out_buf[z] = p_main[pl.ds(PAD + ROWS * (z + 3) + 4, 32)]
-    out_copy = pltpu.make_async_copy(out_buf, out_hbm, out_sem)
-    out_copy.start()
+        out_ref[z] = p_main[pl.ds(PAD + ROWS * (z + 3) + 4, 32)]
 
     at = iota(1, (1, LANES)) // 32
     mine = jnp.zeros((1, LANES), jnp.float32)
@@ -568,7 +609,6 @@
     ]
     for i in range(ITERS):
         hist_ref[i] = jnp.sum(jnp.sqrt(squares[i + 1] / squares[0]))
-    out_copy.wait()
     for copy in started:
         copy.wait_send()
 
@@ -584,15 +624,15 @@
     n_first = n_dirs + 4
     scratch = [
         vmem(8, 32, LANES), vmem(8, 32, LANES), vmem(8, 32, LANES),
-        pltpu.VMEM((32, LANES), jnp.int32), vmem(8, 32, LANES),
-        vmem(2, 8, 8, LANES), vmem(2, ROWS, LANES),
+        pltpu.VMEM((32, LANES), jnp.int32),
+        vmem(2, 8, 8, LANES), vmem(2, ROWS, LANES), vmem(2, 2, 16, LANES),
         vmem(2, 3, 32, LANES), vmem(2, 2, 32, LANES), vmem(2, 2, 32, LANES),
         vmem(2, 8, 8, LANES), vmem(2, 2, 3, 8, LANES),
-        vmem(3, 2, ROWS, LANES), vmem(3, 2, 2, 8, LANES),
-        vmem(ITERS, 16, ROWS, LANES),
+        vmem(2, ROWS, LANES), vmem(2, 2, 16, LANES), vmem(3, 2, 2, 8, LANES),
+        vmem(ITERS, 16, ROWS, LANES), vmem(ITERS, 2, 2, 32, LANES), vmem(ITERS, 2, 2, 16, LANES),
         vmem(ITERS, 2, 6, ROWS, LANES), vmem(ITERS, 2, 15, 8, LANES),
-        vmem(ITERS, 2, 2, 6, 8, LANES),
-        vmem(ITERS, 3, 2, ROWS, LANES), vmem(ITERS, 3, 2, 2, 8, LANES),
+        vmem(ITERS, 2, 2, 40, LANES),
+        vmem(ITERS, 2, ROWS, LANES), vmem(ITERS, 2, 2, 16, LANES), vmem(ITERS, 3, 2, 2, 8, LANES),
         vmem(FLAT, LANES), vmem(SIDE, LANES), vmem(SIDE, LANES), vmem(FLAT, LANES), vmem(FLAT, LANES),
         vmem(6, FLAT, LANES), vmem(7, ROWS, LANES), vmem(7, ROWS, LANES),
         vmem(FLAT, LANES), vmem(ROWS, LANES), vmem(ROWS, LANES), vmem(8, ROWS, LANES),
@@ -602,7 +642,7 @@
     scratch += [
         pltpu.VMEM((2 * LANES, 2 * LANES), jnp.bfloat16),
         vmem(2, 8, LANES), vmem(2, 16, 8, LANES),
-        pltpu.SemaphoreType.DMA((4,)), pltpu.SemaphoreType.DMA,
+        pltpu.SemaphoreType.DMA((4,)),
         pltpu.SemaphoreType.DMA((n_first,)), pltpu.SemaphoreType.DMA((n_first,)),
         pltpu.SemaphoreType.DMA((ITERS, n_dirs)), pltpu.SemaphoreType.DMA((ITERS, n_dirs)),
         pltpu.SemaphoreType.DMA((2, 15)), pltpu.SemaphoreType.DMA((2, 15)),
@@ -617,12 +657,12 @@
             ),
             in_specs=[pl.BlockSpec(memory_space=pl.ANY)] * 4,
             out_specs=(
-                pl.BlockSpec(memory_space=pl.ANY),
+                pl.BlockSpec(memory_space=pltpu.VMEM),
                 pl.BlockSpec(memory_space=pltpu.SMEM),
             ),
             scratch_shapes=scratch,
             compiler_params=pltpu.CompilerParams(
-                collective_id=0, has_side_effects=True, vmem_limit_bytes=60 * 2**20
+                collective_id=0, has_side_effects=True, vmem_limit_bytes=55056 * 2**10
             ),
             name="schwarz",
         )(source, permeability, storage, column_depth)

time: 56.8 us -> 53.4 us (0.940)
  Pallas kernels: 53.9 us -> 50.8 us
    pallas_call x1, Pallas kernels: 53.9 us -> 50.8 us  [per_device(): pl.pallas_call(functools.partial(kernel, sizes), out_shape=(jax.ShapeDtyp...]
where the time goes in v4:
time: 53.4 us; the launch traced here: 53.3 us
  Pallas kernels  50.8 us (95%)
  local copies, waits for them, and re-layouts  1.88 us (4%)
  between operations  0.65 us (1%)
    pallas_call x1, Pallas kernels, per_device(): pl.pallas_call(functools.partial(kernel, sizes), out_shape=(jax.ShapeDtyp...  50.8 us
    unnamed x4, local copies, waits for them, and re-layouts  1.88 us

profile of v4, /device:TPU:1, one launch (start us, length us, event | category | flops | bytes accessed | tf_op | source)
XLA Modules:
  0.0 53.3 jit_solution(13070639263829572851)
XLA Ops:
  0.6 0.0 copy-start
  0.6 0.7 %copy-done = s32[32,128]{1,0:T(8,128)S(1)} copy-done((s32[32,128]{1,0:T(8,128)S(1)}, s32[32,128]{1,0:T(8,128)}, u32[]{:S(2)}) %copy-start) | copy-done | bytes 16408
  1.3 50.8 %schwarz.1 = (f32[8,32,128]{2,1,0:T(8,128)S(1)}, f32[3]{0:T(128)S(1)}) custom-call(f32[8,32,128]{2,1,0:T(8,128)} %src_hbm.1, f32[8,32,128]{2,1,0:T(8,128)} %perm_hbm.1, f32[8,32,128]{2,1,0:T(8,128)} %stor_hbm.1, s32[32,128]{1,0:T(8,128)S(1)} %copy-done), custom_call_target="tpu_custom_call" | custom-call | tf_op jit(solution)/shard_map/schwarz/pallas_call | solution.py:652
  52.1 0.7 %copy.8 = f32[8,32,128]{2,1,0:T(8,128)} copy(f32[8,32,128]{2,1,0:T(8,128)S(1)} %get-tuple-element.4) | data formatting | bytes 262144
  52.8 0.5 copy.9
Async XLA Ops:
  0.6 0.7 %copy-start = (s32[32,128]{1,0:T(8,128)S(1)}, s32[32,128]{1,0:T(8,128)}, u32[]{:S(2)}) copy-start(s32[32,128]{1,0:T(8,128)} %depth_hbm.1) | copy-start | bytes 49156

commit v5 on v4

--- a/solution.py
+++ b/solution.py
@@ -1,4 +1,5 @@
 import functools
+import math
 
 import jax
 import jax.numpy as jnp
@@ -103,7 +104,7 @@
     k_main, k_a, k_b, s_main, q_main,
     w_main, w_a, w_b, alpha, alpha_a, alpha_b, scale,
     r0_main, r0_a, r0_b, r_main, r_a, r_b, u_main, u_a, u_b, v_main, v_a, v_b, p_main, p_a, p_b,
-    shifter, part, part_in,
+    shifter, part, part_in, tally,
     load_sem, send0, recv0, sends, recvs, ar_send, ar_recv,
 ):
     n_gx, n_gy, n_gz = sizes
@@ -116,14 +117,21 @@
             lax.rem(gz + s[0] + n_gz, n_gz),
         )
 
+    def wait_rows(sem, rows):
+        span = tally.at[pl.ds(0, rows)]
+        pltpu.make_async_copy(span, span, sem).wait()
+
+    def rows_of(ref):
+        return math.prod(ref.shape[:-1])
+
     barrier = pltpu.get_barrier_semaphore()
     for s in DIRS:
         pl.semaphore_signal(barrier, inc=1, device_id=device(s), device_id_type=MESH)
 
     loads = [
-        pltpu.make_async_copy(a, b, load_sem.at[i])
-        for i, (a, b) in enumerate(
-            ((depth_hbm, in_depth), (perm_hbm, in_perm), (stor_hbm, in_stor), (src_hbm, in_src))
+        pltpu.make_async_copy(a, b, load_sem)
+        for a, b in (
+            (depth_hbm, in_depth), (perm_hbm, in_perm), (stor_hbm, in_stor), (src_hbm, in_src)
         )
     ]
     for copy in loads:
@@ -160,8 +168,7 @@
             jnp.where(lanes_between(at, STEP * z - 5, STEP * z + 1), moved, accs[1]),
         )
 
-    for copy in loads:
-        copy.wait()
+    wait_rows(load_sem, 3 * 8 * 32 + 32)
 
     depth = in_depth[...]
     for z in range(8):
@@ -169,18 +176,14 @@
 
     pl.semaphore_wait(barrier, len(DIRS))
 
-    started = []
-    exchange0 = []
+    rows0 = []
 
     def post0(src, dst, s):
-        i = len(exchange0)
-        copy = pltpu.make_async_remote_copy(
-            src_ref=src, dst_ref=dst, send_sem=send0.at[i], recv_sem=recv0.at[i],
+        pltpu.make_async_remote_copy(
+            src_ref=src, dst_ref=dst, send_sem=send0, recv_sem=recv0,
             device_id=device(s), device_id_type=MESH,
-        )
-        copy.start()
-        exchange0.append(copy)
-        started.append(copy)
+        ).start()
+        rows0.append(rows_of(src))
 
     for sz in (-1, 1):
         u = part_of(sz)
@@ -221,8 +224,7 @@
             post0(own_fold.at[u, d], rzy0.at[u, d], s)
         else:
             post0(own_side.at[d], ry0.at[d], s)
-    for copy in exchange0:
-        copy.wait_recv()
+    wait_rows(recv0, sum(rows0))
 
     def inside(flag):
         return flag.astype(jnp.float32)
@@ -417,20 +419,18 @@
         return value
 
     partials = [total]
+    sent = [(send0, sum(rows0))]
     for k in range(ITERS):
         rhs, rhs_a, rhs_b = (r0_main, r0_a, r0_b) if k == 0 else (r_main, r_a, r_b)
-        copies = []
+        rows = []
         last_one = k == ITERS - 1
 
         def post(source, target, s):
-            i = DIRS.index(s)
-            copy = pltpu.make_async_remote_copy(
-                src_ref=source, dst_ref=target, send_sem=sends.at[k, i], recv_sem=recvs.at[k, i],
+            pltpu.make_async_remote_copy(
+                src_ref=source, dst_ref=target, send_sem=sends.at[k], recv_sem=recvs.at[k],
                 device_id=device(s), device_id_type=MESH,
-            )
-            copy.start()
-            copies.append(copy)
-            started.append(copy)
+            ).start()
+            rows.append(rows_of(source))
 
         for before_ref, after_ref in (((rhs_a, rhs_b), (u_a, u_b)), ((u_a, u_b), (v_a, v_b))):
             after_ref[0][MIDDLE] = side_sweep(before_ref[0], rhs_a, w_a, 4)
@@ -481,8 +481,8 @@
                 post(send.at[k, planes], rz.at[k, part_of(sz), places], (sz, 0, 0))
         for sx in (-1, 1):
             post(send.at[k, pl.ds(1, 15), row_tile(sx)], rx.at[k, part_of(sx)], (0, sx, 0))
-        for copy in copies:
-            copy.wait_recv()
+        wait_rows(recvs.at[k], sum(rows))
+        sent.append((sends.at[k], sum(rows)))
 
         def edge_rows(u, v, i):
             at = iota(0, (8, LANES))
@@ -587,19 +587,15 @@
     for n, targets in enumerate(rounds):
         here = part_in.at[n, slots[n], pl.ds(0, 1)]
         part[n, 0:1] = mine
-        copies = []
-        for i, target in enumerate(targets):
-            copy = pltpu.make_async_remote_copy(
+        for target in targets:
+            pltpu.make_async_remote_copy(
                 src_ref=part.at[n, pl.ds(0, 1)], dst_ref=here,
-                send_sem=ar_send.at[n, i], recv_sem=ar_recv.at[n, i],
+                send_sem=ar_send.at[n], recv_sem=ar_recv.at[n],
                 device_id=target, device_id_type=MESH,
-            )
-            copy.start()
-            copies.append(copy)
-            started.append(copy)
+            ).start()
         here[...] = mine
-        for copy in copies:
-            copy.wait_recv()
+        wait_rows(ar_recv.at[n], len(targets))
+        sent.append((ar_send.at[n], len(targets)))
         terms = [part_in[n, i, 0:1] for i in range(len(targets) + 1)]
         while len(terms) > 1:
             terms = [sum(terms[i + 1 : i + 2], terms[i]) for i in range(0, len(terms), 2)]
@@ -609,8 +605,8 @@
     ]
     for i in range(ITERS):
         hist_ref[i] = jnp.sum(jnp.sqrt(squares[i + 1] / squares[0]))
-    for copy in started:
-        copy.wait_send()
+    for sem, rows in sent:
+        wait_rows(sem, rows)
 
 
 def solution(mesh):
@@ -620,8 +616,6 @@
     def vmem(*shape):
         return pltpu.VMEM(shape, f32)
 
-    n_dirs = len(DIRS)
-    n_first = n_dirs + 4
     scratch = [
         vmem(8, 32, LANES), vmem(8, 32, LANES), vmem(8, 32, LANES),
         pltpu.VMEM((32, LANES), jnp.int32),
@@ -642,10 +636,10 @@
     scratch += [
         pltpu.VMEM((2 * LANES, 2 * LANES), jnp.bfloat16),
         vmem(2, 8, LANES), vmem(2, 16, 8, LANES),
-        pltpu.SemaphoreType.DMA((4,)),
-        pltpu.SemaphoreType.DMA((n_first,)), pltpu.SemaphoreType.DMA((n_first,)),
-        pltpu.SemaphoreType.DMA((ITERS, n_dirs)), pltpu.SemaphoreType.DMA((ITERS, n_dirs)),
-        pltpu.SemaphoreType.DMA((2, 15)), pltpu.SemaphoreType.DMA((2, 15)),
+        vmem(2048, LANES),
+        pltpu.SemaphoreType.DMA, pltpu.SemaphoreType.DMA, pltpu.SemaphoreType.DMA,
+        pltpu.SemaphoreType.DMA((ITERS,)), pltpu.SemaphoreType.DMA((ITERS,)),
+        pltpu.SemaphoreType.DMA((2,)), pltpu.SemaphoreType.DMA((2,)),
     ]
 
     def per_device(source, permeability, storage, column_depth):

time: 53.4 us -> 50.8 us (0.951)
  Pallas kernels: 50.8 us -> 48.1 us
    pallas_call x1, Pallas kernels: 50.8 us -> 48.1 us  [per_device(): pl.pallas_call(functools.partial(kernel, sizes), out_shape=(jax.ShapeDtyp...]
where the time goes in v5:
time: 50.8 us; the launch traced here: 50.6 us
  Pallas kernels  48.1 us (95%)
  local copies, waits for them, and re-layouts  1.88 us (4%)
  between operations  0.65 us (1%)
    pallas_call x1, Pallas kernels, per_device(): pl.pallas_call(functools.partial(kernel, sizes), out_shape=(jax.ShapeDtyp...  48.1 us
    unnamed x4, local copies, waits for them, and re-layouts  1.88 us

profile of v5, /device:TPU:1, one launch (start us, length us, event | category | flops | bytes accessed | tf_op | source)
XLA Modules:
  0.0 50.6 jit_solution(3603534988407308866)
XLA Ops:
  0.6 0.0 copy-start
  0.6 0.7 %copy-done = s32[32,128]{1,0:T(8,128)S(1)} copy-done((s32[32,128]{1,0:T(8,128)S(1)}, s32[32,128]{1,0:T(8,128)}, u32[]{:S(2)}) %copy-start) | copy-done | bytes 16408
  1.3 48.1 %schwarz.1 = (f32[8,32,128]{2,1,0:T(8,128)S(1)}, f32[3]{0:T(128)S(1)}) custom-call(f32[8,32,128]{2,1,0:T(8,128)} %src_hbm.1, f32[8,32,128]{2,1,0:T(8,128)} %perm_hbm.1, f32[8,32,128]{2,1,0:T(8,128)} %stor_hbm.1, s32[32,128]{1,0:T(8,128)S(1)} %copy-done), custom_call_target="tpu_custom_call" | custom-call | tf_op jit(solution)/shard_map/schwarz/pallas_call | solution.py:646
  49.4 0.7 %copy.8 = f32[8,32,128]{2,1,0:T(8,128)} copy(f32[8,32,128]{2,1,0:T(8,128)S(1)} %get-tuple-element.4) | data formatting | bytes 262144
  50.1 0.5 %copy.9 = f32[3]{0:T(128)} copy(f32[3]{0:T(128)S(1)} %get-tuple-element.5) | data formatting | bytes 24
Async XLA Ops:
  0.6 0.7 %copy-start = (s32[32,128]{1,0:T(8,128)S(1)}, s32[32,128]{1,0:T(8,128)}, u32[]{:S(2)}) copy-start(s32[32,128]{1,0:T(8,128)} %depth_hbm.1) | copy-start | bytes 49156

commit v6 on v5

--- a/solution.py
+++ b/solution.py
@@ -64,8 +64,8 @@
     return z, u - STEP * z
 
 
-def row_tile(sx):
-    return {0: pl.ds(0, ROWS), 1: pl.ds(ROWS - 8, 8), -1: pl.ds(0, 8)}[sx]
+def strip(sx):
+    return pl.ds(1 if sx > 0 else 2, 5)
 
 
 def add_tiles(acc, first, last):
@@ -124,6 +124,7 @@
     def rows_of(ref):
         return math.prod(ref.shape[:-1])
 
+    rxy0[...] = jnp.zeros(rxy0.shape, jnp.float32)
     barrier = pltpu.get_barrier_semaphore()
     for s in DIRS:
         pl.semaphore_signal(barrier, inc=1, device_id=device(s), device_id_type=MESH)
@@ -138,6 +139,8 @@
         copy.start()
 
     zero_plane = jnp.zeros((ROWS, LANES), jnp.float32)
+    for ref in (rz, rxy, rx):
+        ref[...] = jnp.zeros(ref.shape, jnp.float32)
     own_rows[...] = jnp.zeros(own_rows.shape, jnp.float32)
     own_side[...] = jnp.zeros(own_side.shape, jnp.float32)
     for ref in (k_main, s_main, q_main):
@@ -215,11 +218,17 @@
         u, v, d = part_of(sz), part_of(sx), part_of(sy)
         if sy == 0:
             if sz == 0:
-                post0(own_rows.at[v], rx0.at[v], s)
+                post0(own_rows.at[v, :, pl.ds(0, 7)], rx0.at[v, :, pl.ds(0, 7)], s)
             elif sx != 0:
-                post0(own_rows.at[v, pl.ds(5 * u, 3)], rzx0.at[u, v], s)
+                post0(
+                    own_rows.at[v, pl.ds(5 * u, 3), pl.ds(0, 7)],
+                    rzx0.at[u, v, :, pl.ds(0, 7)], s,
+                )
         elif sx != 0:
-            post0(own_side.at[d, row_tile(sx)], rxy0.at[sz + 1, v, d], s)
+            post0(
+                own_side.at[d, pl.ds(33 if v else 4, 3)],
+                rxy0.at[sz + 1, v, d, pl.ds(1 if v else 4, 3)], s,
+            )
         elif sz != 0:
             post0(own_fold.at[u, d], rzy0.at[u, d], s)
         else:
@@ -450,7 +459,10 @@
             u, v, d = part_of(sz), part_of(sx), part_of(sy)
             if sy != 0:
                 if sx != 0:
-                    post(send.at[k, 14 + d, row_tile(sx)], rxy.at[k, sz + 1, v, d], s)
+                    post(
+                        send.at[k, 14 + d, pl.ds(33 if v else 2, 5)],
+                        rxy.at[k, sz + 1, v, d, strip(sx)], s,
+                    )
                 elif sz != 0:
                     post(fold_out.at[k, u, d], rzy.at[k, u, d], s)
                 else:
@@ -470,17 +482,24 @@
                 skip = 6 - count if sz > 0 else 0
                 planes, places = pl.ds((8 if sz > 0 else 0) + skip, count), pl.ds(skip, count)
                 u = part_of(sz)
+                pieces = pl.ds(2 + 5 * skip, 5 * count)
                 for v, low in ((0, 2), (1, 33)):
-                    for i in range(6):
+                    for i in range(skip, skip + count):
                         zx_out[k, u, v, 2 + 5 * i : 7 + 5 * i] = send[
                             k, (8 + i) if u else i, low : low + 5
                         ]
                     post(
-                        zx_out.at[k, u, v], rzx.at[k, u, v, pl.ds(0, 32)], (sz, 2 * v - 1, 0)
+                        zx_out.at[k, u, v, pieces], rzx.at[k, u, v, pieces],
+                        (sz, 2 * v - 1, 0),
                     )
-                post(send.at[k, planes], rz.at[k, part_of(sz), places], (sz, 0, 0))
+                kept = pl.ds(2, 36)
+                post(send.at[k, planes, kept], rz.at[k, u, places, kept], (sz, 0, 0))
         for sx in (-1, 1):
-            post(send.at[k, pl.ds(1, 15), row_tile(sx)], rx.at[k, part_of(sx)], (0, sx, 0))
+            v = part_of(sx)
+            post(
+                send.at[k, pl.ds(1, 15), pl.ds(33 if v else 2, 5)],
+                rx.at[k, v, :, strip(sx)], (0, sx, 0),
+            )
         wait_rows(recvs.at[k], sum(rows))
         sent.append((sends.at[k], sum(rows)))
 

time: 50.8 us -> 49.1 us (0.967)
  Pallas kernels: 48.1 us -> 46.5 us
    pallas_call x1, Pallas kernels: 48.1 us -> 46.5 us  [per_device(): pl.pallas_call(functools.partial(kernel, sizes), out_shape=(jax.ShapeDtyp...]
where the time goes in v6:
time: 49.1 us; the launch traced here: 49 us
  Pallas kernels  46.5 us (95%)
  local copies, waits for them, and re-layouts  1.88 us (4%)
  between operations  0.65 us (1%)
    pallas_call x1, Pallas kernels, per_device(): pl.pallas_call(functools.partial(kernel, sizes), out_shape=(jax.ShapeDtyp...  46.5 us
    unnamed x4, local copies, waits for them, and re-layouts  1.88 us

profile of v6, /device:TPU:1, one launch (start us, length us, event | category | flops | bytes accessed | tf_op | source)
XLA Modules:
  0.0 49.0 jit_solution(1567051682209153676)
XLA Ops:
  0.6 0.0 copy-start
  0.6 0.7 %copy-done = s32[32,128]{1,0:T(8,128)S(1)} copy-done((s32[32,128]{1,0:T(8,128)S(1)}, s32[32,128]{1,0:T(8,128)}, u32[]{:S(2)}) %copy-start) | copy-done | bytes 16408
  1.3 46.5 %schwarz.1 = (f32[8,32,128]{2,1,0:T(8,128)S(1)}, f32[3]{0:T(128)S(1)}) custom-call(f32[8,32,128]{2,1,0:T(8,128)} %src_hbm.1, f32[8,32,128]{2,1,0:T(8,128)} %perm_hbm.1, f32[8,32,128]{2,1,0:T(8,128)} %stor_hbm.1, s32[32,128]{1,0:T(8,128)S(1)} %copy-done), custom_call_target="tpu_custom_call" | custom-call | tf_op jit(solution)/shard_map/schwarz/pallas_call | solution.py:665
  47.8 0.7 %copy.8 = f32[8,32,128]{2,1,0:T(8,128)} copy(f32[8,32,128]{2,1,0:T(8,128)S(1)} %get-tuple-element.4) | data formatting | bytes 262144
  48.5 0.5 %copy.9 = f32[3]{0:T(128)} copy(f32[3]{0:T(128)S(1)} %get-tuple-element.5) | data formatting | bytes 24
Async XLA Ops:
  0.6 0.7 %copy-start = (s32[32,128]{1,0:T(8,128)S(1)}, s32[32,128]{1,0:T(8,128)}, u32[]{:S(2)}) copy-start(s32[32,128]{1,0:T(8,128)} %depth_hbm.1) | copy-start | bytes 49156

commit v7 on v6

--- a/solution.py
+++ b/solution.py
@@ -177,22 +177,6 @@
     for z in range(8):
         in_perm[z] = jnp.where((gz * 8 + z) < depth, in_perm[z], 0.0)
 
-    pl.semaphore_wait(barrier, len(DIRS))
-
-    rows0 = []
-
-    def post0(src, dst, s):
-        pltpu.make_async_remote_copy(
-            src_ref=src, dst_ref=dst, send_sem=send0, recv_sem=recv0,
-            device_id=device(s), device_id_type=MESH,
-        ).start()
-        rows0.append(rows_of(src))
-
-    for sz in (-1, 1):
-        u = part_of(sz)
-        post0(in_perm.at[pl.ds(5 * u, 3)], rz_k.at[u], (sz, 0, 0))
-        post0(in_stor.at[pl.ds(6 * u, 2)], rz_s.at[u], (sz, 0, 0))
-        post0(in_src.at[pl.ds(6 * u, 2)], rz_q.at[u], (sz, 0, 0))
     zero_block = jnp.zeros((32, LANES), jnp.float32)
     edges = [(zero_block, zero_block)] * 3
     for z in range(8):
@@ -213,6 +197,22 @@
     for d in range(2):
         for u in range(2):
             own_fold[u, d] = fold(own_side[d], STEP * (8 if u else 3) - (1 if d else 4))
+    pl.semaphore_wait(barrier, len(DIRS))
+
+    rows0 = []
+
+    def post0(src, dst, s):
+        pltpu.make_async_remote_copy(
+            src_ref=src, dst_ref=dst, send_sem=send0, recv_sem=recv0,
+            device_id=device(s), device_id_type=MESH,
+        ).start()
+        rows0.append(rows_of(src))
+
+    for sz in (-1, 1):
+        u = part_of(sz)
+        post0(in_perm.at[pl.ds(5 * u, 3)], rz_k.at[u], (sz, 0, 0))
+        post0(in_stor.at[pl.ds(6 * u, 2)], rz_s.at[u], (sz, 0, 0))
+        post0(in_src.at[pl.ds(6 * u, 2)], rz_q.at[u], (sz, 0, 0))
     for s in DIRS:
         sz, sx, sy = s
         u, v, d = part_of(sz), part_of(sx), part_of(sy)
@@ -588,21 +588,24 @@
     def ring(i, n):
         return min(i, n - i)
 
+    chips = sorted(
+        (
+            (i, j, h)
+            for i in range(n_gx)
+            for j in range(n_gy // 2)
+            for h in range(n_gz)
+            if (i, j, h) != (0, 0, 0)
+        ),
+        key=lambda t: -ring(t[0], n_gx) - ring(t[1], n_gy // 2) - ring(t[2], n_gz),
+    )
     rounds = (
-        sorted(
-            ((i, h) for i in range(n_gx) for h in range(2) if (i, h) != (0, 0)),
-            key=lambda t: -ring(t[0], n_gx) - 0.3 * t[1],
-        ),
-        sorted(
-            ((i, h) for i in range(n_gy // 2) for h in range(n_gz) if (i, h) != (0, 0)),
-            key=lambda t: -ring(t[0], n_gy // 2) - ring(t[1], n_gz),
-        ),
-    )
-    rounds = (
-        [(lax.rem(gx + i, n_gx), gy if h == 0 else pair, gz) for i, h in rounds[0]],
-        [(gx, lax.rem(gy + 2 * i, n_gy), lax.rem(gz + h, n_gz)) for i, h in rounds[1]],
-    )
-    slots = (gx * 2 + lax.rem(gy, 2), (gy // 2) * n_gz + gz)
+        [(gx, pair, gz)],
+        [
+            (lax.rem(gx + i, n_gx), lax.rem(gy + 2 * j, n_gy), lax.rem(gz + h, n_gz))
+            for i, j, h in chips
+        ],
+    )
+    slots = (lax.rem(gy, 2), (gx * (n_gy // 2) + gy // 2) * n_gz + gz)
     for n, targets in enumerate(rounds):
         here = part_in.at[n, slots[n], pl.ds(0, 1)]
         part[n, 0:1] = mine
@@ -654,7 +657,7 @@
         scratch += [vmem(FLAT, LANES), vmem(SIDE, LANES), vmem(SIDE, LANES)]
     scratch += [
         pltpu.VMEM((2 * LANES, 2 * LANES), jnp.bfloat16),
-        vmem(2, 8, LANES), vmem(2, 16, 8, LANES),
+        vmem(2, 8, LANES), vmem(2, 128, 8, LANES),
         vmem(2048, LANES),
         pltpu.SemaphoreType.DMA, pltpu.SemaphoreType.DMA, pltpu.SemaphoreType.DMA,
         pltpu.SemaphoreType.DMA((ITERS,)), pltpu.SemaphoreType.DMA((ITERS,)),

time: 49.1 us -> 48.4 us (0.986)
  Pallas kernels: 46.5 us -> 45.7 us
    pallas_call x1, Pallas kernels: 46.5 us -> 45.7 us  [per_device(): pl.pallas_call(functools.partial(kernel, sizes), out_shape=(jax.ShapeDtyp...]
where the time goes in v7:
time: 48.4 us; the launch traced here: 48.2 us
  Pallas kernels  45.7 us (94%)
  local copies, waits for them, and re-layouts  1.88 us (4%)
  between operations  0.65 us (1%)
    pallas_call x1, Pallas kernels, per_device(): pl.pallas_call(functools.partial(kernel, sizes), out_shape=(jax.ShapeDtyp...  45.7 us
    unnamed x4, local copies, waits for them, and re-layouts  1.88 us

profile of v7, /device:TPU:1, one launch (start us, length us, event | category | flops | bytes accessed | tf_op | source)
XLA Modules:
  0.0 48.2 jit_solution(13767999530106851731)
XLA Ops:
  0.6 0.0 copy-start
  0.6 0.7 %copy-done = s32[32,128]{1,0:T(8,128)S(1)} copy-done((s32[32,128]{1,0:T(8,128)S(1)}, s32[32,128]{1,0:T(8,128)}, u32[]{:S(2)}) %copy-start) | copy-done | bytes 16408
  1.3 45.7 %schwarz.1 = (f32[8,32,128]{2,1,0:T(8,128)S(1)}, f32[3]{0:T(128)S(1)}) custom-call(f32[8,32,128]{2,1,0:T(8,128)} %src_hbm.1, f32[8,32,128]{2,1,0:T(8,128)} %perm_hbm.1, f32[8,32,128]{2,1,0:T(8,128)} %stor_hbm.1, s32[32,128]{1,0:T(8,128)S(1)} %copy-done), custom_call_target="tpu_custom_call" | custom-call | tf_op jit(solution)/shard_map/schwarz/pallas_call | solution.py:668
  47.1 0.7 %copy.8 = f32[8,32,128]{2,1,0:T(8,128)} copy(f32[8,32,128]{2,1,0:T(8,128)S(1)} %get-tuple-element.4) | data formatting | bytes 262144
  47.7 0.5 %copy.9 = f32[3]{0:T(128)} copy(f32[3]{0:T(128)S(1)} %get-tuple-element.5) | data formatting | bytes 24
Async XLA Ops:
  0.6 0.7 %copy-start = (s32[32,128]{1,0:T(8,128)S(1)}, s32[32,128]{1,0:T(8,128)}, u32[]{:S(2)}) copy-start(s32[32,128]{1,0:T(8,128)} %depth_hbm.1) | copy-start | bytes 49156

commit v8 on v7

--- a/solution.py
+++ b/solution.py
@@ -64,8 +64,8 @@
     return z, u - STEP * z
 
 
-def strip(sx):
-    return pl.ds(1 if sx > 0 else 2, 5)
+def strip(sx, count, first=0):
+    return pl.ds(first + (6 - count if sx > 0 else 2), count)
 
 
 def add_tiles(acc, first, last):
@@ -433,6 +433,7 @@
         rhs, rhs_a, rhs_b = (r0_main, r0_a, r0_b) if k == 0 else (r_main, r_a, r_b)
         rows = []
         last_one = k == ITERS - 1
+        width, head = (3, 4) if last_one else (5, 2)
 
         def post(source, target, s):
             pltpu.make_async_remote_copy(
@@ -460,8 +461,8 @@
             if sy != 0:
                 if sx != 0:
                     post(
-                        send.at[k, 14 + d, pl.ds(33 if v else 2, 5)],
-                        rxy.at[k, sz + 1, v, d, strip(sx)], s,
+                        send.at[k, 14 + d, strip(sx, width, 32 * v)],
+                        rxy.at[k, sz + 1, v, d, strip(sx, width)], s,
                     )
                 elif sz != 0:
                     post(fold_out.at[k, u, d], rzy.at[k, u, d], s)
@@ -482,31 +483,34 @@
                 skip = 6 - count if sz > 0 else 0
                 planes, places = pl.ds((8 if sz > 0 else 0) + skip, count), pl.ds(skip, count)
                 u = part_of(sz)
-                pieces = pl.ds(2 + 5 * skip, 5 * count)
-                for v, low in ((0, 2), (1, 33)):
+                pieces = pl.ds(head + width * skip, width * count)
+                for v, low in ((0, 2), (1, 38 - width)):
                     for i in range(skip, skip + count):
-                        zx_out[k, u, v, 2 + 5 * i : 7 + 5 * i] = send[
-                            k, (8 + i) if u else i, low : low + 5
+                        place = head + width * i
+                        zx_out[k, u, v, place : place + width] = send[
+                            k, (8 + i) if u else i, low : low + width
                         ]
                     post(
                         zx_out.at[k, u, v, pieces], rzx.at[k, u, v, pieces],
                         (sz, 2 * v - 1, 0),
                     )
-                kept = pl.ds(2, 36)
+                kept = pl.ds(3, 34) if last_one else pl.ds(2, 36)
                 post(send.at[k, planes, kept], rz.at[k, u, places, kept], (sz, 0, 0))
         for sx in (-1, 1):
             v = part_of(sx)
             post(
-                send.at[k, pl.ds(1, 15), pl.ds(33 if v else 2, 5)],
-                rx.at[k, v, :, strip(sx)], (0, sx, 0),
+                send.at[k, pl.ds(1, 15), strip(sx, width, 32 * v)],
+                rx.at[k, v, :, strip(sx, width)], (0, sx, 0),
             )
         wait_rows(recvs.at[k], sum(rows))
         sent.append((sends.at[k], sum(rows)))
 
         def edge_rows(u, v, i):
             at = iota(0, (8, LANES))
-            tile = rzx[k, u, v, 5 * i + v : 5 * i + v + 8]
-            return jnp.where(between(at, 2 - v, 6 - v), tile, 0.0)
+            first = 6 - width if v else 2
+            start = head + width * i - first
+            tile = rzx[k, u, v, start : start + 8]
+            return jnp.where(between(at, first, first + width - 1), tile, 0.0)
 
         new_p = []
         for own, d, offset, shift, y, low, high, outer_low, outer_high, ref in (
@@ -574,9 +578,6 @@
             total = total + value * value
         partials.append(total)
 
-    for z in range(8):
-        out_ref[z] = p_main[pl.ds(PAD + ROWS * (z + 3) + 4, 32)]
-
     at = iota(1, (1, LANES)) // 32
     mine = jnp.zeros((1, LANES), jnp.float32)
     for i, value in enumerate(partials):
@@ -598,10 +599,13 @@
         ),
         key=lambda t: -ring(t[0], n_gx) - ring(t[1], n_gy // 2) - ring(t[2], n_gz),
     )
+    at_x = [lax.rem(gx + i, n_gx) for i in range(n_gx)]
+    at_y = [lax.rem(gy + 2 * i, n_gy) for i in range(n_gy // 2)]
+    at_z = [lax.rem(gz + i, n_gz) for i in range(n_gz)]
     rounds = (
         [(gx, pair, gz)],
         [
-            (lax.rem(gx + i, n_gx), lax.rem(gy + 2 * j, n_gy), lax.rem(gz + h, n_gz))
+            (at_x[i], at_y[j], at_z[h])
             for i, j, h in chips
         ],
     )
@@ -616,6 +620,9 @@
                 device_id=target, device_id_type=MESH,
             ).start()
         here[...] = mine
+        if n == 1:
+            for z in range(8):
+                out_ref[z] = p_main[pl.ds(PAD + ROWS * (z + 3) + 4, 32)]
         wait_rows(ar_recv.at[n], len(targets))
         sent.append((ar_send.at[n], len(targets)))
         terms = [part_in[n, i, 0:1] for i in range(len(targets) + 1)]

time: 48.4 us -> 48.1 us (level)
  no operation moved by 1% of the time
where the time goes in v8:
time: 48.1 us; the launch traced here: 47.9 us
  Pallas kernels  45.4 us (94%)
  local copies, waits for them, and re-layouts  1.88 us (4%)
  between operations  0.65 us (1%)
    pallas_call x1, Pallas kernels, per_device(): pl.pallas_call(functools.partial(kernel, sizes), out_shape=(jax.ShapeDtyp...  45.4 us
    unnamed x4, local copies, waits for them, and re-layouts  1.88 us

profile of v8, /device:TPU:1, one launch (start us, length us, event | category | flops | bytes accessed | tf_op | source)
XLA Modules:
  0.0 47.9 jit_solution(13313929131214942443)
XLA Ops:
  0.6 0.0 copy-start
  0.6 0.7 %copy-done = s32[32,128]{1,0:T(8,128)S(1)} copy-done((s32[32,128]{1,0:T(8,128)S(1)}, s32[32,128]{1,0:T(8,128)}, u32[]{:S(2)}) %copy-start) | copy-done | bytes 16408
  1.3 45.4 %schwarz.1 = (f32[8,32,128]{2,1,0:T(8,128)S(1)}, f32[3]{0:T(128)S(1)}) custom-call(f32[8,32,128]{2,1,0:T(8,128)} %src_hbm.1, f32[8,32,128]{2,1,0:T(8,128)} %perm_hbm.1, f32[8,32,128]{2,1,0:T(8,128)} %stor_hbm.1, s32[32,128]{1,0:T(8,128)S(1)} %copy-done), custom_call_target="tpu_custom_call" | custom-call | tf_op jit(solution)/shard_map/schwarz/pallas_call | solution.py:675
  46.8 0.7 %copy.8 = f32[8,32,128]{2,1,0:T(8,128)} copy(f32[8,32,128]{2,1,0:T(8,128)S(1)} %get-tuple-element.4) | data formatting | bytes 262144
  47.4 0.5 %copy.9 = f32[3]{0:T(128)} copy(f32[3]{0:T(128)S(1)} %get-tuple-element.5) | data formatting | bytes 24
Async XLA Ops:
  0.6 0.7 %copy-start = (s32[32,128]{1,0:T(8,128)S(1)}, s32[32,128]{1,0:T(8,128)}, u32[]{:S(2)}) copy-start(s32[32,128]{1,0:T(8,128)} %depth_hbm.1) | copy-start | bytes 49156
